TPU v7x, 128 devices: a whole 4x4x4 slice. The times are simulated.
128 devices in a mesh: axial: 4 (over z), sector: 16 (over y_lo, x, core), modes: 2 (over y_hi).
Axes of the slice: x: 4, y: 4 (y_hi: 2, y_lo: 2; y = y_hi * 2 + y_lo), z: 4, core: 2. Of those that a mesh axis runs over, the one named last changes fastest.
Arguments:
- rhs: float32 [2, 8, 64, 128, 256], P(None, 'modes', 'axial', 'sector'), may hold values from -8 to 8
- adjoint_start: float32 [2, 8, 64, 128, 256], P(None, 'modes', 'axial', 'sector'), may hold values from -8 to 8
- sound_sq: float32 [64, 128, 256], P('axial', 'sector'), may hold values from 0.25 to 4
- direct_mode: bfloat16 [2, 8, 64, 128, 256], P(None, 'modes', 'axial', 'sector'), may hold values from -6 to 6
- omega_sq: float32 [2, 8], P(None, 'modes'), may hold values from 0.5 to 3
- flame_gain: float32 [4, 8192], P('axial', 'sector'), may hold values from 1 to 8
- delay_phase: float32 [8, 32], P('modes'), may hold values from -3.140625 to 3.140625
- delay_bin: int32 [4, 8192], P('axial', 'sector'), may hold values from 0 to 31
- flame_cell: int32 [4, 8192], P('axial', 'sector'), may hold values from 0 to 32767
- injector_sector: int32 [4, 8192, 1], P('axial', 'sector'), may hold values from 0 to 15; in each aligned block of 512 rows (0 to 511, 512 to 1023, ..., all dimensions but the last counted through in order) at most 96 rows name the same one
- injector_cell: int32 [4, 8192], P('axial', 'sector'), may hold values from 0 to 32767
Outputs:
- adjoint: float32 [2, 8, 64, 128, 256], P(None, 'modes', 'axial', 'sector')
- sensitivity: float32 [64, 128, 256], P('axial', 'sector')
Inputs may be any that keep to these rules, and one draw needn't show every extreme that they name: `injector_sector`: among the flame cells of one device (each aligned block of 512 along 8192), at most 96 name the same sector, a bound that some block reaches.
All inputs are finite; a program needn't handle non-finite values.
Results may differ from a plain program's by a relative error of at most 0.0003.
Values sent between devices are 32-bit elements; how exact they have to be, the bound alone decides.
A program may use at most 128 MiB of HBM per device.

v0:
```python
import jax
import jax.numpy as jnp
from jax import lax
from jax.sharding import PartitionSpec as P

ITERS = 2


relax_weight = 0.6


def with_halo(block, sides, width, periodic):
    for axis, dim in sides:
        count = lax.axis_size(axis)
        forward = [(i, i + 1) for i in range(count - 1)]
        if periodic:
            forward.append((count - 1, 0))
        backward = [(target, source) for source, target in forward]
        low = lax.ppermute(
            lax.slice_in_dim(block, block.shape[dim] - width, None, axis=dim), axis, forward
        )
        high = lax.ppermute(lax.slice_in_dim(block, 0, width, axis=dim), axis, backward)
        block = jnp.concatenate([low, block, high], axis=dim)
    return block


def couple(values, speeds, val_alo, val_ahi, spd_alo, spd_ahi, val_slo, val_shi, spd_slo, spd_shi):
    k_alo = 0.5 * (speeds + spd_alo)
    k_ahi = 0.5 * (speeds + spd_ahi)
    k_slo = 0.5 * (speeds + spd_slo)
    k_shi = 0.5 * (speeds + spd_shi)
    applied = k_alo * (values - val_alo) + k_ahi * (values - val_ahi)
    applied = applied + k_slo * (values - val_slo) + k_shi * (values - val_shi)
    weights = k_alo + k_ahi + k_slo + k_shi
    k_radial = 0.5 * (speeds[..., 1:] + speeds[..., :-1])
    radial_flux = k_radial * (values[..., 1:] - values[..., :-1])
    value_lo = [(0, 0)] * (values.ndim - 1) + [(1, 0)]
    value_hi = [(0, 0)] * (values.ndim - 1) + [(0, 1)]
    speed_lo = [(0, 0)] * (speeds.ndim - 1) + [(1, 0)]
    speed_hi = [(0, 0)] * (speeds.ndim - 1) + [(0, 1)]
    applied = applied + jnp.pad(radial_flux, value_lo) - jnp.pad(radial_flux, value_hi)
    weights = weights + jnp.pad(k_radial, speed_lo) + jnp.pad(k_radial, speed_hi)
    return (applied, weights)


def pick_cells(field_rows, cell_ids):
    flat_rows = field_rows.reshape(field_rows.shape[0], -1)
    return jnp.take(flat_rows, cell_ids, axis=1)


def add_cells(totals, amounts, cell_ids):
    block_shape = totals.shape
    flat_totals = totals.reshape(block_shape[0], -1)
    return flat_totals.at[:, cell_ids].add(amounts).reshape(block_shape)


def local(
    rhs,
    adjoint_start,
    sound_sq,
    direct_mode,
    omega_sq,
    flame_gain,
    delay_phase,
    delay_bin,
    flame_cell,
    injector_sector,
    injector_cell,
):
    group_modes = rhs.shape[1]
    channels = 2 * group_modes
    axial_cells, azimuth_cells, radial_cells = sound_sq.shape
    row_count = axial_cells * azimuth_cells
    flame_count = flame_cell.shape[1]
    bin_count = delay_phase.shape[1]
    my_sector = lax.axis_index("sector")
    sources = flame_cell[0]
    targets = injector_sector[0, :, 0]
    dest_cells = injector_cell[0]
    gains = flame_gain[0][None, :]
    bin_table = (delay_bin[0][:, None] == jnp.arange(bin_count, dtype=jnp.int32)[None, :]).astype(
        jnp.float32
    )
    cosines = jnp.dot(jnp.cos(delay_phase), bin_table.T, precision=lax.Precision.HIGHEST)
    sines = jnp.dot(-jnp.sin(delay_phase), bin_table.T, precision=lax.Precision.HIGHEST)
    w_real = omega_sq[0][:, None, None, None]
    w_imag = omega_sq[1][:, None, None, None]
    fields = adjoint_start
    for step_index in range(ITERS):
        layered = jnp.concatenate(
            [fields.reshape(channels, axial_cells, azimuth_cells, radial_cells), sound_sq[None]], 0
        )
        axial_ext = with_halo(layered, (("axial", 1),), 1, False)
        sector_ext = with_halo(layered, (("sector", 2),), 1, True)
        values = layered[:-1]
        applied, weights = couple(
            values,
            sound_sq,
            axial_ext[:-1, :-2],
            axial_ext[:-1, 2:],
            axial_ext[-1, :-2],
            axial_ext[-1, 2:],
            sector_ext[:-1, :, :-2],
            sector_ext[:-1, :, 2:],
            sector_ext[-1, :, :-2],
            sector_ext[-1, :, 2:],
        )
        applied = applied.reshape(2, group_modes, axial_cells, azimuth_cells, radial_cells)
        field_rows = fields.reshape(channels, row_count, radial_cells)
        picked = pick_cells(field_rows, sources).reshape(2, group_modes, flame_count)
        real_part = gains * (cosines * picked[0] - sines * picked[1])
        imag_part = gains * (cosines * picked[1] + sines * picked[0])
        contributions = jnp.concatenate([real_part, imag_part], 0).T
        empty_totals = jnp.zeros((channels, row_count, radial_cells), jnp.float32)
        portion_values = lax.all_gather(contributions, "sector", axis=0, tiled=True)
        portion_targets = lax.all_gather(targets, "sector", axis=0, tiled=True)
        portion_cells = lax.all_gather(dest_cells, "sector", axis=0, tiled=True)
        owned = jnp.where((portion_targets == my_sector)[:, None], portion_values, 0.0)
        totals = add_cells(empty_totals, owned.T, portion_cells)
        injected = totals.reshape(2, group_modes, axial_cells, azimuth_cells, radial_cells)
        mass_real = w_real * fields[0] - w_imag * fields[1]
        mass_imag = w_real * fields[1] + w_imag * fields[0]
        operated = applied - jnp.stack([mass_real, mass_imag]) + injected
        fields = fields + relax_weight * (rhs - operated) / weights
    direct_values = direct_mode.astype(jnp.float32)
    partial_terms = jnp.sum(fields[0] * direct_values[0] - fields[1] * direct_values[1], axis=0)
    sensitivity = lax.psum(partial_terms, "modes")
    return (fields, sensitivity)


def solution(mesh):
    placed = (
        P(None, "modes", "axial", "sector", None),
        P(None, "modes", "axial", "sector", None),
        P("axial", "sector", None),
        P(None, "modes", "axial", "sector", None),
        P(None, "modes"),
        P("axial", "sector"),
        P("modes", None),
        P("axial", "sector"),
        P("axial", "sector"),
        P("axial", "sector", None),
        P("axial", "sector"),
    )
    return jax.shard_map(
        local,
        mesh=mesh,
        in_specs=placed,
        out_specs=(P(None, "modes", "axial", "sector", None), P("axial", "sector", None)),
        check_vma=False,
    )
```

profile of v0, /device:TPU:1, one launch (start us, length us, event | category | flops | bytes accessed | tf_op | source)
XLA Modules:
  0.0 327.4 jit_solution(9883875618179850261)
XLA Ops:
  7.3 2.7 fusion.45
  10.0 2.6 collective-permute-start.2
  14.1 4.2 %collective-permute-start = (f32[9,1,8,256]{3,2,1,0:T(8,128)}, f32[9,1,8,256]{3,2,1,0:T(8,128)}, u32[]{:S(2)}, u32[]{:S(2)}) collective-permute-start(f32[9,1,8,256]{3,2,1,0:T(8,128)} %get-tuple-element.23), channel_id=1, source_target_pairs={{0,32},{32,64},{64,96},{1,33},{33,65},{65,97},{2,34},{34,66},{66,9... | collective-permute-start | bytes 221192 | tf_op jit(solution)/shard_map/ppermute | solution.py:19
  20.0 20.5 %all-gather = s32[1,8192]{1,0:T(1,128)S(1)} all-gather(s32[1,512]{1,0:T(1,128)S(1)} %copy-done.25), channel_id=2, replica_groups=mesh['axial'=4,'sector'=16,'modes'=2] {'sector'}, dimensions={1}, use_global_device_ids=true | all-gather | bytes 34816 | tf_op jit(solution)/shard_map/all_gather | solution.py:117
  40.5 8.9 %copy.21 = f32[8,32768]{0,1:T(8,128)} copy(f32[8,32768]{1,0:T(8,128)S(1)} %reshape_reshape.12) | data formatting | bytes 2097152 | tf_op jit(solution)/shard_map/reshape;reshape | solution.py:47
  49.9 6.8 %gather_fusion = f32[512,8]{1,0:T(8,128)S(1)} fusion(f32[8,32768]{0,1:T(8,128)} %copy.21, s32[1024]{0:T(1024)S(1)} %pad_clamp_fusion), kind=kCustom, calls=%fused_computation.clone | custom fusion | bytes 34816 | tf_op jit(solution)/shard_map/jit(_take)/gather | solution.py:48
  58.1 17.0 %all_gather.16 = f32[8192,8]{0,1:T(8,128)S(1)} all-gather(f32[512,8]{0,1:T(8,128)S(1)} %maximum_bitcast_fusion), channel_id=1, replica_groups=mesh['axial'=4,'sector'=16,'modes'=2] {'sector'}, dimensions={0}, use_global_device_ids=true | all-gather | bytes 278528 | tf_op jit(solution)/shard_map/all_gather | solution.py:115
  75.1 17.6 %all-gather.1 = s32[1,8192,1]{1,2,0:T(1,128)S(1)} all-gather(s32[1,512,1]{1,2,0:T(1,128)S(1)} %copy-done.26), channel_id=3, replica_groups=mesh['axial'=4,'sector'=16,'modes'=2] {'sector'}, dimensions={1}, use_global_device_ids=true | all-gather | bytes 34816 | tf_op jit(solution)/shard_map/all_gather | solution.py:116
  94.5 2.6 copy.23
  97.1 51.1 %scatter_custom_fusion = f32[8,32768]{0,1:T(8,128)} fusion(s32[8192]{0:T(1024)S(1)} %compare_select_fusion, f32[8192,8]{1,0:T(8,128)} %copy.23, f32[]{:T(128)} %constant.3.clone.1), kind=kCustom, calls=%fused_computation.6 | custom fusion | flops 65536 | bytes 1049088 | tf_op jit(solution)/shard_map/scatter-add | solution.py:54
  148.2 9.7 %copy.24 = f32[8,32768]{1,0:T(8,128)S(1)} copy(f32[8,32768]{0,1:T(8,128)} %scatter_custom_fusion) | data formatting | bytes 2097152 | tf_op jit(solution)/shard_map/scatter-add | solution.py:54
  161.2 1.6 fusion.6
  168.2 9.1 %copy.25 = f32[8,32768]{0,1:T(8,128)} copy(f32[8,32768]{1,0:T(8,128)} %reshape_reshape.14) | data formatting | bytes 2097152 | tf_op jit(solution)/shard_map/reshape;reshape | solution.py:47
  177.3 7.4 %gather_fusion.1 = f32[512,8]{1,0:T(8,128)} fusion(f32[8,32768]{0,1:T(8,128)} %copy.25, s32[1024]{0:T(1024)S(1)} %copy-done.14), kind=kCustom, calls=%fused_computation.1.clone | custom fusion | bytes 34816 | tf_op jit(solution)/shard_map/jit(_take)/gather | solution.py:48
  185.8 17.0 %all_gather.17 = f32[8192,8]{0,1:T(8,128)S(1)} all-gather(f32[512,8]{0,1:T(8,128)S(1)} %maximum_bitcast_fusion.1), channel_id=1, replica_groups=mesh['axial'=4,'sector'=16,'modes'=2] {'sector'}, dimensions={0}, use_global_device_ids=true | all-gather | bytes 278528 | tf_op jit(solution)/shard_map/all_gather | solution.py:115
  203.6 3.5 %copy.27 = f32[8192,8]{1,0:T(8,128)} copy(f32[8192,8]{0,1:T(8,128)} %broadcast_select_fusion) | data formatting | bytes 524288 | tf_op jit(solution)/shard_map/jit(_where)/select_n | solution.py:118
  207.1 51.1 %scatter_custom_fusion.1 = f32[8,32768]{0,1:T(8,128)} fusion(s32[8192]{0:T(1024)} %copy-done.12, f32[8192,8]{1,0:T(8,128)} %copy.27, f32[]{:T(128)} %constant.3.clone.1), kind=kCustom, calls=%fused_computation.4 | custom fusion | flops 65536 | bytes 1049088 | tf_op jit(solution)/shard_map/scatter-add | solution.py:54
  258.1 9.8 %copy.28 = f32[8,32768]{1,0:T(8,128)} copy(f32[8,32768]{0,1:T(8,128)} %scatter_custom_fusion.1) | data formatting | bytes 2097152 | tf_op jit(solution)/shard_map/scatter-add | solution.py:54
  269.5 4.3 %collective-permute-start.4 = (f32[9,1,8,256]{3,2,1,0:T(8,128)}, f32[9,1,8,256]{3,2,1,0:T(8,128)S(1)}, u32[]{:S(2)}, u32[]{:S(2)}) collective-permute-start(f32[9,1,8,256]{3,2,1,0:T(8,128)} %get-tuple-element.15), channel_id=1, source_target_pairs={{0,32},{32,64},{64,96},{1,33},{33,65},{65,97},{2,34},{34,66},{66,9... | collective-permute-start | bytes 221192 | tf_op jit(solution)/shard_map/ppermute | solution.py:19
  275.3 1.8 collective-permute-start.6
  277.1 1.8 collective-permute-done.5
  279.2 2.8 collective-permute-done.7
  286.1 32.9 %all-reduce.8.cloned.1.call-done = f32[16,8,256]{2,1,0:T(8,128)} async-done(((f32[16,8,256]{2,1,0:T(8,128)}), f32[16,8,256]{2,1,0:T(8,128)}) %all-reduce.8.cloned.1.call-update) | async-done | bytes 131088 | tf_op jit(solution)/shard_map/psum | solution.py:127
  319.0 1.6 copy.32
  (116 shorter events, 24.8 us)
Async XLA Ops:
  7.2 311.9 %all-reduce.8.cloned.1.call-start = ((), (), s32[]{:S(2)}) async-start(), calls=%async_computation | async-start | bytes 262144 | tf_op jit(solution)/shard_map/psum | solution.py:127
  7.2 12.6 %copy-start.1 = (f32[16,8,256]{2,1,0:T(8,128)S(1)}, f32[16,8,256]{2,1,0:T(8,128)}, u32[]{:S(2)}) copy-start(f32[16,8,256]{2,1,0:T(8,128)} %param.15) | copy-start | bytes 393220
  7.2 12.7 %copy-start.25 = (s32[1,512]{1,0:T(1,128)S(1)}, s32[1,512]{1,0:T(1,128)}, u32[]{:S(2)}) copy-start(s32[1,512]{1,0:T(1,128)} %param.23) | copy-start | bytes 6148
  10.0 151.2 %collective-permute-start.2 = (f32[9,16,1,256]{3,2,1,0:T(1,128)}, f32[9,16,1,256]{3,2,1,0:T(1,128)S(1)}, u32[]{:S(2)}, u32[]{:S(2)}) collective-permute-start(f32[9,16,1,256]{3,2,1,0:T(1,128)} %get-tuple-element.27), channel_id=1, source_target_pairs={{0,2},{2,4},{4,6},{6,8},{8,10},{10,12},{12,14},{14,16},{16,18},{18... | collective-permute-start | bytes 442376 | tf_op jit(solution)/shard_map/ppermute | solution.py:19
  12.6 148.6 %collective-permute-start.3 = (f32[9,16,1,256]{3,2,1,0:T(1,128)}, f32[9,16,1,256]{3,2,1,0:T(1,128)}, u32[]{:S(2)}, u32[]{:S(2)}) collective-permute-start(f32[9,16,1,256]{3,2,1,0:T(1,128)} %get-tuple-element.28), channel_id=1, source_target_pairs={{2,0},{4,2},{6,4},{8,6},{10,8},{12,10},{14,12},{16,14},{18,16},{20... | collective-permute-start | bytes 442376 | tf_op jit(solution)/shard_map/ppermute | solution.py:22
  14.1 145.9 %collective-permute-start = (f32[9,1,8,256]{3,2,1,0:T(8,128)}, f32[9,1,8,256]{3,2,1,0:T(8,128)}, u32[]{:S(2)}, u32[]{:S(2)}) collective-permute-start(f32[9,1,8,256]{3,2,1,0:T(8,128)} %get-tuple-element.23), channel_id=1, source_target_pairs={{0,32},{32,64},{64,96},{1,33},{33,65},{65,97},{2,34},{34,66},{66,9... | collective-permute-start | bytes 221192 | tf_op jit(solution)/shard_map/ppermute | solution.py:19
  18.3 141.8 %collective-permute-start.1 = (f32[9,1,8,256]{3,2,1,0:T(8,128)}, f32[9,1,8,256]{3,2,1,0:T(8,128)}, u32[]{:S(2)}, u32[]{:S(2)}) collective-permute-start(f32[9,1,8,256]{3,2,1,0:T(8,128)} %get-tuple-element.24), channel_id=1, source_target_pairs={{32,0},{64,32},{96,64},{33,1},{65,33},{97,65},{34,2},{66,34},{98,6... | collective-permute-start | bytes 221192 | tf_op jit(solution)/shard_map/ppermute | solution.py:22
  19.8 37.3 %copy-start.19 = (pred[512]{0:T(512)(128)(4,1)}, pred[512]{0:T(512)(128)(4,1)S(1)}, u32[]{:S(2)}) copy-start(pred[512]{0:T(512)(128)(4,1)S(1)} %compare_and_fusion) | copy-start | bytes 1540
  40.5 16.4 %copy-start.30 = (s32[1,512]{1,0:T(1,128)S(1)}, s32[1,512]{1,0:T(1,128)}, u32[]{:S(2)}) copy-start(s32[1,512]{1,0:T(1,128)} %param.20) | copy-start | bytes 6148
  40.5 16.4 %copy-start.31 = (f32[4,32]{1,0:T(4,128)S(1)}, f32[4,32]{1,0:T(4,128)}, u32[]{:S(2)}) copy-start(f32[4,32]{1,0:T(4,128)} %param.19) | copy-start | bytes 1540
  40.5 16.7 %copy-start.27 = (f32[1,512]{1,0:T(1,128)S(1)}, f32[1,512]{1,0:T(1,128)}, u32[]{:S(2)}) copy-start(f32[1,512]{1,0:T(1,128)} %param.18) | copy-start | bytes 6148
  40.5 34.6 %copy-start.26 = (s32[1,512,1]{1,2,0:T(1,128)S(1)}, s32[1,512,1]{1,2,0:T(1,128)}, u32[]{:S(2)}) copy-start(s32[1,512,1]{1,2,0:T(1,128)} %param.22) | copy-start | bytes 6148
  49.3 43.8 %copy-start.29 = (f32[2,4]{1,0:T(2,128)S(1)}, f32[2,4]{1,0:T(2,128)}, u32[]{:S(2)}) copy-start(f32[2,4]{1,0:T(2,128)} %param.17) | copy-start | bytes 100
  57.2 37.3 %copy-start.15 = (f32[4,512]{1,0:T(4,128)}, f32[4,512]{1,0:T(4,128)S(1)}, u32[]{:S(2)}) copy-start(f32[4,512]{1,0:T(4,128)S(1)} %convolution_bitcast_fusion.1) | copy-start | bytes 24580
  168.1 17.6 %copy-start.20 = (pred[512]{0:T(512)(128)(4,1)S(1)}, pred[512]{0:T(512)(128)(4,1)}, u32[]{:S(2)}) copy-start(pred[512]{0:T(512)(128)(4,1)} %copy-done.19) | copy-start | bytes 1540
  168.1 17.6 %copy-start.16 = (f32[4,512]{1,0:T(4,128)S(1)}, f32[4,512]{1,0:T(4,128)}, u32[]{:S(2)}) copy-start(f32[4,512]{1,0:T(4,128)} %copy-done.15) | copy-start | bytes 24580
  168.1 17.6 %copy-start.17 = (f32[4,512]{1,0:T(4,128)S(1)}, f32[4,512]{1,0:T(4,128)}, u32[]{:S(2)}) copy-start(f32[4,512]{1,0:T(4,128)} %get-tuple-element.39) | copy-start | bytes 24580
  168.1 17.6 %copy-start.28 = (f32[1,512]{1,0:T(1,128)S(1)}, f32[1,512]{1,0:T(1,128)}, u32[]{:S(2)}) copy-start(f32[1,512]{1,0:T(1,128)} %param.18) | copy-start | bytes 6148
  168.2 34.7 %copy-start.11 = (pred[8192]{0:T(1024)(128)(4,1)S(1)}, pred[8192]{0:T(1024)(128)(4,1)}, u32[]{:S(2)}) copy-start(pred[8192]{0:T(1024)(128)(4,1)} %copy-done.10) | copy-start | bytes 24580
  269.5 7.6 %collective-permute-start.4 = (f32[9,1,8,256]{3,2,1,0:T(8,128)}, f32[9,1,8,256]{3,2,1,0:T(8,128)S(1)}, u32[]{:S(2)}, u32[]{:S(2)}) collective-permute-start(f32[9,1,8,256]{3,2,1,0:T(8,128)} %get-tuple-element.15), channel_id=1, source_target_pairs={{0,32},{32,64},{64,96},{1,33},{33,65},{65,97},{2,34},{34,66},{66,9... | collective-permute-start | bytes 221192 | tf_op jit(solution)/shard_map/ppermute | solution.py:19
  273.7 5.1 %collective-permute-start.5 = (f32[9,1,8,256]{3,2,1,0:T(8,128)S(1)}, f32[9,1,8,256]{3,2,1,0:T(8,128)S(1)}, u32[]{:S(2)}, u32[]{:S(2)}) collective-permute-start(f32[9,1,8,256]{3,2,1,0:T(8,128)S(1)} %get-tuple-element.16), channel_id=1, source_target_pairs={{32,0},{64,32},{96,64},{33,1},{65,33},{97,65},{34,2},{66,34},{98,6... | collective-permute-start | bytes 221192 | tf_op jit(solution)/shard_map/ppermute | solution.py:22
  275.3 3.9 %collective-permute-start.6 = (f32[9,16,1,256]{3,2,1,0:T(1,128)S(1)}, f32[9,16,1,256]{3,2,1,0:T(1,128)S(1)}, u32[]{:S(2)}, u32[]{:S(2)}) collective-permute-start(f32[9,16,1,256]{3,2,1,0:T(1,128)S(1)} %get-tuple-element.19), channel_id=1, source_target_pairs={{0,2},{2,4},{4,6},{6,8},{8,10},{10,12},{12,14},{14,16},{16,18},{18... | collective-permute-start | bytes 442376 | tf_op jit(solution)/shard_map/ppermute | solution.py:19
  277.1 4.9 %collective-permute-start.7 = (f32[9,16,1,256]{3,2,1,0:T(1,128)S(1)}, f32[9,16,1,256]{3,2,1,0:T(1,128)S(1)}, u32[]{:S(2)}, u32[]{:S(2)}) collective-permute-start(f32[9,16,1,256]{3,2,1,0:T(1,128)S(1)} %get-tuple-element.20), channel_id=1, source_target_pairs={{2,0},{4,2},{6,4},{8,6},{10,8},{12,10},{14,12},{16,14},{18,16},{20... | collective-permute-start | bytes 442376 | tf_op jit(solution)/shard_map/ppermute | solution.py:22
  285.1 35.5 %copy-start.3 = (f32[2,4,16,8,256]{4,3,2,1,0:T(8,128)}, f32[2,4,16,8,256]{4,3,2,1,0:T(8,128)S(1)}, u32[]{:S(2)}) copy-start(f32[2,4,16,8,256]{4,3,2,1,0:T(8,128)S(1)} %fusion.41) | copy-start | bytes 3145732
  (17 other events, 59.8 us)
Sparse Core Ops, SparseCore 0:
  286.3 32.7 all-reduce.7
where the time goes:
time: 328 us; the launch traced here: 327 us
  other arithmetic  120 us (37%)
  blocking collectives  72.1 us (22%)
  local copies, waits for them, and re-layouts  67 us (20%)
  waiting for transfers between devices  37.6 us (11%)
  starting transfers between devices  15.4 us (5%)
  between operations  14.5 us (4%)
    scatter-add x2, other arithmetic, add_cells(): return flat_totals.at[:, cell_ids].add(amounts).reshape(block_shape)  102 us
    all_gather x2, blocking collectives, local(): portion_values = lax.all_gather(contributions, 'sector', axis=0, tiled=True)  34 us
    psum x1, waiting for transfers between devices, local(): sensitivity = lax.psum(partial_terms, 'modes')  32.9 us
    all_gather x1, blocking collectives, local(): portion_cells = lax.all_gather(dest_cells, 'sector', axis=0, tiled=True)  20.5 us
    scatter-add x2, local copies, waits for them, and re-layouts, add_cells(): return flat_totals.at[:, cell_ids].add(amounts).reshape(block_shape)  19.4 us
    another operation x4, local copies, waits for them, and re-layouts, pick_cells(): flat_rows = field_rows.reshape(field_rows.shape[0], -1)  19.3 us
    all_gather x1, blocking collectives, local(): portion_targets = lax.all_gather(targets, 'sector', axis=0, tiled=True)  17.6 us
    gather x4, local copies, waits for them, and re-layouts, pick_cells(): return jnp.take(flat_rows, cell_ids, axis=1)  15.3 us
  transfers between devices with their start and end apart: 9, of which 4 were waited for; matrix products, arithmetic and copies ran while one was open for 27% of the time, Pallas kernels for 0%

commit v1 on v0

v1 whole, which is shorter than its diff:
```python
import functools

import jax
import jax.numpy as jnp
from jax import lax
from jax.experimental import pallas as pl
from jax.experimental.pallas import tpu as pltpu
from jax.sharding import PartitionSpec as P

ITERS = 2
RELAX = 0.6
CAP = 96
LANES = 128
MESH = pl.DeviceIdType.MESH
BF16 = jnp.bfloat16
F32 = jnp.float32
I32 = jnp.int32


def one_hot(flags):
    return jnp.where(flags, 1.0, 0.0).astype(BF16)


def halves(values):
    high = values.astype(BF16)
    return high, (values - high.astype(F32)).astype(BF16)


def dot_nt(left, right):
    return lax.dot_general(
        left, right, (((1,), (1,)), ((), ())), preferred_element_type=F32
    )


def read(ref, *index):
    *lead, at = index
    tiles = ref.shape[len(lead)]
    return jnp.concatenate([ref[(*lead, i, at)] for i in range(tiles)], axis=-1)


def write(ref, *index_and_value):
    *lead, at, value = index_and_value
    for i in range(ref.shape[len(lead)]):
        ref[(*lead, i, at)] = value[..., i * LANES : (i + 1) * LANES]


def kernel(
    n_sector,
    n_axial,
    shape,
    rhs_hbm,
    start_hbm,
    sound_hbm,
    direct_hbm,
    omega_hbm,
    gain_hbm,
    phase_hbm,
    bin_hbm,
    source_hbm,
    sector_hbm,
    target_hbm,
    adjoint_hbm,
    sens_hbm,
    rhs,
    field_a,
    field_b,
    sound,
    direct,
    omega,
    gain,
    phase,
    bins,
    source,
    sector,
    target,
    result,
    base,
    coef,
    edge,
    pick_radial,
    pick_row,
    lane_hot,
    dist_hot,
    gain_cos,
    gain_sin,
    put_row,
    put_radial,
    sound_send,
    sound_side,
    side_send,
    side_recv,
    cell_send,
    cell_recv,
    flame_send,
    flame_recv,
    sens_own,
    sens_other,
    in_sem,
    out_sem,
    sound_sems,
    halo_sems,
    cell_sems,
    flame_sems,
    sens_sems,
):
    modes, axial_cells, azimuth_cells, radial_cells = shape
    channels = 2 * modes
    rows = axial_cells * azimuth_cells
    flames = gain.shape[1]
    slots = n_sector * CAP
    tiles = radial_cells // LANES
    axial = lax.axis_index("axial")
    my_sector = lax.axis_index("sector")
    my_modes = lax.axis_index("modes")
    up_axial = lax.rem(axial + 1, n_axial)
    down_axial = lax.rem(axial + n_axial - 1, n_axial)

    def sector_at(distance):
        return lax.rem(my_sector + (distance + n_sector), n_sector)

    barrier = pltpu.get_barrier_semaphore()
    for distance in range(1, n_sector):
        pl.semaphore_signal(
            barrier, inc=1, device_id={"sector": sector_at(distance)}, device_id_type=MESH
        )
    for other in (up_axial, down_axial):
        pl.semaphore_signal(barrier, inc=1, device_id={"axial": other}, device_id_type=MESH)
    pl.semaphore_signal(
        barrier, inc=1, device_id={"modes": 1 - my_modes}, device_id_type=MESH
    )

    inner = pl.ds(azimuth_cells, rows)
    loads = [
        pltpu.make_async_copy(a, b, in_sem.at[i])
        for i, (a, b) in enumerate(
            (
                (sector_hbm, sector),
                (target_hbm, target),
                (source_hbm, source),
                (bin_hbm, bins),
                (phase_hbm, phase),
                (gain_hbm, gain),
                (sound_hbm.at[:, pl.ds(0, LANES)], sound.at[0, inner]),
                (sound_hbm.at[:, pl.ds(LANES, LANES)], sound.at[1, inner]),
                (start_hbm.at[:, :, pl.ds(0, LANES)], field_a.at[:, 0, inner]),
                (start_hbm.at[:, :, pl.ds(LANES, LANES)], field_a.at[:, 1, inner]),
                (omega_hbm, omega),
                (rhs_hbm, rhs),
                (direct_hbm, direct),
            )
        )
    ]
    for load in loads:
        load.start()

    for load in loads[:3]:
        load.wait()
    distance_of = lax.rem(sector[...] - my_sector + n_sector, n_sector)
    to_sector = jnp.broadcast_to(distance_of, (n_sector, flames)) == lax.broadcasted_iota(
        I32, (n_sector, flames), 0
    )
    dist_f32 = jnp.where(to_sector, 1.0, 0.0)
    dist_hot[...] = dist_f32
    before = one_hot(
        lax.broadcasted_iota(I32, (flames, flames), 0)
        < lax.broadcasted_iota(I32, (flames, flames), 1)
    )
    earlier = jnp.dot(dist_f32.astype(BF16), before, preferred_element_type=F32)
    rank = jnp.sum(dist_f32 * earlier, axis=0, keepdims=True).astype(I32)
    lane = (rank + CAP * distance_of) & (LANES - 1)
    lane_hot[...] = one_hot(
        lax.broadcasted_iota(I32, (LANES, flames), 0) == jnp.broadcast_to(lane, (LANES, flames))
    )

    def pack(parts):
        left = jnp.concatenate(
            [
                jnp.concatenate(
                    [part * dist_hot[d : d + 1, :] for d in range(n_sector)], axis=0
                ).astype(BF16)
                for part in parts
            ],
            axis=0,
        )
        packed = dot_nt(left, lane_hot[...])
        total = packed[: 8 * n_sector]
        for i in range(1, len(parts)):
            total = total + packed[8 * n_sector * i : 8 * n_sector * (i + 1)]
        return total.reshape(n_sector, 8, LANES)

    target_row = (target[...] // radial_cells).astype(F32)
    target_radial = (target[...] % radial_cells).astype(F32)
    sub = lax.broadcasted_iota(I32, (8, flames), 0)
    cell_send[...] = pack(
        [
            jnp.where(
                sub == 0,
                jnp.broadcast_to(target_row, (8, flames)),
                jnp.where(sub == 1, jnp.broadcast_to(target_radial, (8, flames)), 0.0),
            )
        ]
    )

    loads[6].wait()
    loads[7].wait()
    for side, row in ((0, 0), (1, azimuth_cells - 1)):
        for i in range(tiles):
            sound_send[side, i] = sound[i, pl.ds(azimuth_cells + row, axial_cells, azimuth_cells), :]

    pl.semaphore_wait(barrier, n_sector + 2)

    def axial_halo(ref, sems):
        last = pl.ds(rows, azimuth_cells)
        first = pl.ds(azimuth_cells, azimuth_cells)
        below = pl.ds(0, azimuth_cells)
        above = pl.ds(rows + azimuth_cells, azimuth_cells)
        at = (lambda part: ref.at[:, part]) if len(ref.shape) == 3 else (lambda part: ref.at[:, :, part])
        return [
            pltpu.make_async_remote_copy(
                src_ref=at(last),
                dst_ref=at(below),
                send_sem=sems.at[0, 0],
                recv_sem=sems.at[1, 0],
                device_id={"axial": up_axial},
                device_id_type=MESH,
            ),
            pltpu.make_async_remote_copy(
                src_ref=at(first),
                dst_ref=at(above),
                send_sem=sems.at[0, 1],
                recv_sem=sems.at[1, 1],
                device_id={"axial": down_axial},
                device_id_type=MESH,
            ),
        ]

    def side_halo(send, recv, sems):
        return [
            pltpu.make_async_remote_copy(
                src_ref=send.at[1],
                dst_ref=recv.at[0],
                send_sem=sems.at[0, 2],
                recv_sem=sems.at[1, 2],
                device_id={"sector": sector_at(1)},
                device_id_type=MESH,
            ),
            pltpu.make_async_remote_copy(
                src_ref=send.at[0],
                dst_ref=recv.at[1],
                send_sem=sems.at[0, 3],
                recv_sem=sems.at[1, 3],
                device_id={"sector": sector_at(-1)},
                device_id_type=MESH,
            ),
        ]

    def blocks(send, recv, sems):
        return [
            pltpu.make_async_remote_copy(
                src_ref=send.at[distance],
                dst_ref=recv.at[distance],
                send_sem=sems.at[0, distance],
                recv_sem=sems.at[1, distance],
                device_id={"sector": sector_at(distance)},
                device_id_type=MESH,
            )
            for distance in range(1, n_sector)
        ]

    sends = []

    def start(copies):
        for copy in copies:
            copy.start()
        sends.extend(copies)
        return copies

    sound_copies = start(axial_halo(sound, sound_sems) + side_halo(sound_send, sound_side, sound_sems))
    cell_copies = start(blocks(cell_send, cell_recv, cell_sems))
    cell_recv[0] = cell_send[0]

    def send_sides(field, step):
        for side, row in ((0, 0), (1, azimuth_cells - 1)):
            for c in range(channels):
                for i in range(tiles):
                    side_send[step, side, c, i] = field[
                        c, i, pl.ds(azimuth_cells + row, axial_cells, azimuth_cells), :
                    ]
        sems = halo_sems.at[step]
        return start(
            axial_halo(field, sems) + side_halo(side_send.at[step], side_recv.at[step], sems)
        )

    cell = source[...]
    row_of = jnp.broadcast_to(cell // radial_cells, (rows, flames))
    pick_row[...] = jnp.where(lax.broadcasted_iota(I32, (rows, flames), 0) == row_of, 1.0, 0.0)
    radial_of = jnp.broadcast_to(cell % radial_cells, (radial_cells, flames))
    radial_hot = one_hot(lax.broadcasted_iota(I32, (radial_cells, flames), 0) == radial_of)
    pick_radial[:radial_cells] = radial_hot
    pick_radial[radial_cells:] = radial_hot

    for load in loads[3:6]:
        load.wait()
    bin_count = phase.shape[1]
    bin_hot = jnp.where(
        lax.broadcasted_iota(I32, (bin_count, flames), 0)
        == jnp.broadcast_to(bins[...], (bin_count, flames)),
        1.0,
        0.0,
    )
    angle = phase[...]
    gains = jnp.broadcast_to(gain[...], (modes, flames))
    exact = lax.Precision.HIGHEST
    gain_cos[...] = gains * jnp.dot(
        jnp.cos(angle), bin_hot, precision=exact, preferred_element_type=F32
    )
    gain_sin[...] = -gains * jnp.dot(
        jnp.sin(angle), bin_hot, precision=exact, preferred_element_type=F32
    )

    def send_flames(field, step):
        group = channels // 2
        picked = []
        for g in range(2):
            values = jnp.concatenate(
                [read(field, g * group + c, pl.ds(azimuth_cells, rows)) for c in range(group)], axis=0
            )
            high, low = halves(values)
            columns = jnp.dot(
                jnp.concatenate([high, low], axis=1), pick_radial[...], preferred_element_type=F32
            ).reshape(group, rows, flames)
            picked.append(jnp.sum(columns * pick_row[...][None], axis=1))
        real, imag = picked
        cosines, sines = gain_cos[...], gain_sin[...]
        amounts = jnp.concatenate(
            [cosines * real - sines * imag, cosines * imag + sines * real], axis=0
        )
        high = amounts.astype(BF16).astype(F32)
        flame_send[step] = pack([high, amounts - high])
        copies = start(blocks(flame_send.at[step], flame_recv.at[step], flame_sems.at[step]))
        flame_recv[step, 0] = flame_send[step, 0]
        return copies

    def squeeze(recv):
        lanes = lax.broadcasted_iota(I32, (8, LANES), 1)
        tiles = []
        for first in range(0, n_sector, 4):
            b = [recv[first + i] for i in range(4)]
            tiles.append(jnp.where(lanes < 96, b[0], b[1]))
            tiles.append(jnp.where(lanes < 64, b[1], b[2]))
            tiles.append(jnp.where(lanes < 32, b[2], b[3]))
        return jnp.concatenate(tiles, axis=1)

    loads[8].wait()
    loads[9].wait()
    halo_copies = send_sides(field_a, 0)
    flame_copies = send_flames(field_a, 0)

    first_axial = axial == 0
    last_axial = axial == n_axial - 1
    for copy in sound_copies:
        copy.wait_recv()
    low_pad = pl.ds(0, azimuth_cells)
    high_pad = pl.ds(rows + azimuth_cells, azimuth_cells)
    sound[:, low_pad, :] = jnp.where(first_axial, 0.0, sound[:, low_pad, :])
    sound[:, high_pad, :] = jnp.where(last_axial, 0.0, sound[:, high_pad, :])
    tile = (azimuth_cells, radial_cells)
    azimuth = lax.broadcasted_iota(I32, tile, 0)
    radial = lax.broadcasted_iota(I32, tile, 1)

    def one_coef(a, _):
        here = pl.multiple_of(a * azimuth_cells, azimuth_cells)
        s = read(sound, pl.ds(here + azimuth_cells, azimuth_cells))
        k_alo = 0.5 * (s + read(sound, pl.ds(here, azimuth_cells)))
        k_ahi = 0.5 * (s + read(sound, pl.ds(here + 2 * azimuth_cells, azimuth_cells)))
        side_lo = jnp.broadcast_to(read(sound_side, 0, pl.ds(a, 1)), tile)
        side_hi = jnp.broadcast_to(read(sound_side, 1, pl.ds(a, 1)), tile)
        k_slo = 0.5 * (s + jnp.where(azimuth == 0, side_lo, pltpu.roll(s, 1, 0)))
        k_shi = 0.5 * (
            s + jnp.where(azimuth == azimuth_cells - 1, side_hi, pltpu.roll(s, azimuth_cells - 1, 0))
        )
        k_rlo = jnp.where(radial == 0, 0.0, 0.5 * (s + pltpu.roll(s, 1, 1)))
        k_rhi = jnp.where(
            radial == radial_cells - 1, 0.0, 0.5 * (s + pltpu.roll(s, radial_cells - 1, 1))
        )
        scale = RELAX / (k_alo + k_ahi + k_slo + k_shi + k_rlo + k_rhi)
        at = pl.ds(here, azimuth_cells)
        coef[0, at, :] = scale
        coef[1, at, :] = scale * k_alo
        coef[2, at, :] = scale * k_ahi
        k_slo = scale * k_slo
        k_shi = scale * k_shi
        coef[3, at, :] = jnp.where(azimuth == 0, 0.0, k_slo)
        coef[4, at, :] = jnp.where(azimuth == azimuth_cells - 1, 0.0, k_shi)
        coef[5, at, :] = scale * k_rlo
        coef[6, at, :] = scale * k_rhi
        write(edge, 0, pl.ds(a, 1), k_slo[0:1])
        write(edge, 1, pl.ds(a, 1), k_shi[azimuth_cells - 1 : azimuth_cells])
        return 0

    lax.fori_loop(0, axial_cells, one_coef, 0)

    loads[10].wait()
    loads[11].wait()
    omega_real = [omega[0, m] for m in range(modes)]
    omega_imag = [omega[1, m] for m in range(modes)]

    def base_rows(field, a):
        here = pl.multiple_of(a * azimuth_cells, azimuth_cells)
        at = pl.ds(here, azimuth_cells)
        mid = pl.ds(here + azimuth_cells, azimuth_cells)
        top = pl.ds(here + 2 * azimuth_cells, azimuth_cells)
        scale, k_alo, k_ahi, k_slo, k_shi, k_rlo, k_rhi = (coef[i, at, :] for i in range(7))
        for m in range(modes):
            real, imag = read(field, m, mid), read(field, modes + m, mid)
            for c, x, mass in (
                (m, real, omega_real[m] * real - omega_imag[m] * imag),
                (modes + m, imag, omega_real[m] * imag + omega_imag[m] * real),
            ):
                near = k_alo * read(field, c, at) + k_ahi * read(field, c, top)
                near = near + k_slo * pltpu.roll(x, 1, 0)
                near = near + k_shi * pltpu.roll(x, azimuth_cells - 1, 0)
                near = near + k_rlo * pltpu.roll(x, 1, 1)
                near = near + k_rhi * pltpu.roll(x, radial_cells - 1, 1)
                write(base, c, at, (1.0 - RELAX) * x + scale * (rhs[c, at, :] + mass) + near)

    def make_base(field, halo, step):
        lax.fori_loop(1, axial_cells - 1, lambda a, _: (base_rows(field, a), 0)[1], 0)
        for copy in halo:
            copy.wait_recv()
        for c in range(channels):
            field[c, :, low_pad, :] = jnp.where(first_axial, 0.0, field[c, :, low_pad, :])
            field[c, :, high_pad, :] = jnp.where(last_axial, 0.0, field[c, :, high_pad, :])
        base_rows(field, 0)
        base_rows(field, axial_cells - 1)
        for side, row in ((0, 0), (1, azimuth_cells - 1)):
            at = pl.ds(row, axial_cells, azimuth_cells)
            for c in range(channels):
                for i in range(tiles):
                    base[c, i, at, :] = (
                        base[c, i, at, :] + edge[side, i] * side_recv[step, side, c, i]
                    )

    make_base(field_a, halo_copies, 0)

    for copy in cell_copies:
        copy.wait_recv()
    cells = squeeze(cell_recv).astype(I32)
    put_row[...] = one_hot(
        lax.broadcasted_iota(I32, (rows, slots), 0) == jnp.broadcast_to(cells[0:1], (rows, slots))
    )
    put_radial[...] = one_hot(
        lax.broadcasted_iota(I32, (radial_cells, slots), 0)
        == jnp.broadcast_to(cells[1:2], (radial_cells, slots))
    ).T

    chunk = rows // 4

    def flame_parts(copies, step):
        for copy in copies:
            copy.wait_recv()
        return halves(squeeze(flame_recv.at[step]))

    def flame_total(parts, first):
        hot = put_row[first : first + chunk, :]
        left = jnp.concatenate(
            [hot * part[c : c + 1, :] for part in parts for c in range(channels)], axis=0
        )
        totals = jnp.dot(left, put_radial[...], preferred_element_type=F32)
        half = channels * chunk
        return totals[:half] + totals[half:]

    parts = flame_parts(flame_copies, 0)
    for first in range(0, rows, chunk):
        totals = flame_total(parts, first)
        scale = coef[0, first : first + chunk, :]
        for c in range(channels):
            write(
                field_b,
                c,
                pl.ds(first + azimuth_cells, chunk),
                read(base, c, pl.ds(first, chunk)) - scale * totals[c * chunk : (c + 1) * chunk],
            )

    halo_copies = send_sides(field_b, 1)
    flame_copies = send_flames(field_b, 1)
    make_base(field_b, halo_copies, 1)
    parts = flame_parts(flame_copies, 1)
    loads[12].wait()
    sens_copies = []
    stores = []
    for i, first in enumerate(range(0, rows, chunk)):
        totals = flame_total(parts, first)
        at = pl.ds(first, chunk)
        scale = coef[0, at, :]
        sens = jnp.zeros((chunk, radial_cells), F32)
        for c in range(channels):
            x = read(base, c, at) - scale * totals[c * chunk : (c + 1) * chunk]
            result[c, at, :] = x
            term = x * direct[c, at, :].astype(F32)
            sens = sens + term if c < modes else sens - term
        sens_own[at, :] = sens
        sens_copies += start(
            [
                pltpu.make_async_remote_copy(
                    src_ref=sens_own.at[at],
                    dst_ref=sens_other.at[at],
                    send_sem=sens_sems.at[0, i],
                    recv_sem=sens_sems.at[1, i],
                    device_id={"modes": 1 - my_modes},
                    device_id_type=MESH,
                )
            ]
        )
        store = pltpu.make_async_copy(result.at[:, at], adjoint_hbm.at[:, at], out_sem.at[i])
        store.start()
        stores.append(store)
    for i, first in enumerate(range(0, rows, chunk)):
        at = pl.ds(first, chunk)
        sens_copies[i].wait_recv()
        sens_other[at, :] = sens_own[at, :] + sens_other[at, :]
    store = pltpu.make_async_copy(sens_other, sens_hbm, out_sem.at[4])
    store.start()
    stores.append(store)
    for copy in sends:
        copy.wait_send()
    for store in stores:
        store.wait()


def local(
    n_sector,
    n_axial,
    rhs,
    adjoint_start,
    sound_sq,
    direct_mode,
    omega_sq,
    flame_gain,
    delay_phase,
    delay_bin,
    flame_cell,
    injector_sector,
    injector_cell,
):
    parts, modes, axial_cells, azimuth_cells, radial_cells = rhs.shape
    channels = parts * modes
    rows = axial_cells * azimuth_cells
    flames = flame_cell.shape[1]
    slots = n_sector * CAP
    block = (channels, rows, radial_cells)
    tiles = radial_cells // LANES
    padded = (channels, tiles, rows + 2 * azimuth_cells, LANES)
    side = (tiles, axial_cells, LANES)
    plane = (rows, radial_cells)
    dma = pltpu.SemaphoreType.DMA
    vmem = pltpu.VMEM
    scratch = [
        vmem(block, F32),
        vmem(padded, F32),
        vmem(padded, F32),
        vmem(padded[1:], F32),
        vmem(block, BF16),
        pltpu.SMEM((2, modes), F32),
        vmem((1, flames), F32),
        vmem(delay_phase.shape, F32),
        vmem((1, flames), I32),
        vmem((1, flames), I32),
        vmem((1, flames), I32),
        vmem((1, flames), I32),
        vmem(block, F32),
        vmem((channels, tiles, rows, LANES), F32),
        vmem((7,) + plane, F32),
        vmem((2,) + side, F32),
        vmem((2 * radial_cells, flames), BF16),
        vmem((rows, flames), F32),
        vmem((LANES, flames), BF16),
        vmem((n_sector, flames), F32),
        vmem((modes, flames), F32),
        vmem((modes, flames), F32),
        vmem((rows, slots), BF16),
        vmem((slots, radial_cells), BF16),
        vmem((2,) + side, F32),
        vmem((2,) + side, F32),
        vmem((ITERS, 2, channels) + side, F32),
        vmem((ITERS, 2, channels) + side, F32),
        vmem((n_sector, 8, LANES), F32),
        vmem((n_sector, 8, LANES), F32),
        vmem((ITERS, n_sector, 8, LANES), F32),
        vmem((ITERS, n_sector, 8, LANES), F32),
        vmem(plane, F32),
        vmem(plane, F32),
        dma((13,)),
        dma((5,)),
        dma((2, 4)),
        dma((ITERS, 2, 4)),
        dma((2, n_sector)),
        dma((ITERS, 2, n_sector)),
        dma((2, 4)),
    ]
    anywhere = pl.BlockSpec(memory_space=pl.ANY)
    adjoint, sensitivity = pl.pallas_call(
        functools.partial(
            kernel, n_sector, n_axial, (modes, axial_cells, azimuth_cells, radial_cells)
        ),
        out_shape=(jax.ShapeDtypeStruct(block, F32), jax.ShapeDtypeStruct(plane, F32)),
        in_specs=[anywhere] * 11,
        out_specs=(anywhere, anywhere),
        scratch_shapes=scratch,
        compiler_params=pltpu.CompilerParams(
            collective_id=0, has_side_effects=True, vmem_limit_bytes=40 * 1024 * 1024
        ),
        name="helmholtz_steps",
    )(
        rhs.reshape(block),
        adjoint_start.reshape(block),
        sound_sq.reshape(plane),
        direct_mode.reshape(block),
        omega_sq,
        flame_gain,
        delay_phase,
        delay_bin,
        flame_cell,
        injector_sector.reshape(1, flames),
        injector_cell,
    )
    return adjoint.reshape(rhs.shape), sensitivity.reshape(sound_sq.shape)


def solution(mesh):
    placed = (
        P(None, "modes", "axial", "sector", None),
        P(None, "modes", "axial", "sector", None),
        P("axial", "sector", None),
        P(None, "modes", "axial", "sector", None),
        P(None, "modes"),
        P("axial", "sector"),
        P("modes", None),
        P("axial", "sector"),
        P("axial", "sector"),
        P("axial", "sector", None),
        P("axial", "sector"),
    )
    return jax.shard_map(
        functools.partial(local, mesh.shape["sector"], mesh.shape["axial"]),
        mesh=mesh,
        in_specs=placed,
        out_specs=(P(None, "modes", "axial", "sector", None), P("axial", "sector", None)),
        check_vma=False,
    )
```

time: 328 us -> 38.9 us (0.12)
  other arithmetic: 120 us -> 0 us
  blocking collectives: 72.1 us -> 0 us
  local copies, waits for them, and re-layouts: 67 us -> 8.08 us
  waiting for transfers between devices: 37.6 us -> 0 us
  Pallas kernels: 0 us -> 29.8 us
  starting transfers between devices: 15.4 us -> 0 us
  between operations: 14.5 us -> 0.69 us
    scatter-add x2 -> x0, other arithmetic: 102 us -> none  [add_cells(): return flat_totals.at[:, cell_ids].add(amounts).reshape(block_shape)]
    all_gather x4 -> x0, blocking collectives: 72.1 us -> none  [the longest x2 34 us: local(): portion_values = lax.all_gather(contributions, 'sector', axis=0, tiled=True)]
    psum x1 -> x0, waiting for transfers between devices: 32.9 us -> none  [local(): sensitivity = lax.psum(partial_terms, 'modes')]
    pallas_call x0 -> x1, Pallas kernels: none -> 29.8 us  [local(): pl.pallas_call(functools.partial(kernel, n_sector, n_axial, (modes, axial...]
    scatter-add x2 -> x0, local copies, waits for them, and re-layouts: 19.4 us -> none  [add_cells(): return flat_totals.at[:, cell_ids].add(amounts).reshape(block_shape)]
    another operation x4 -> x0, local copies, waits for them, and re-layouts: 19.3 us -> none  [pick_cells(): flat_rows = field_rows.reshape(field_rows.shape[0], -1)]
    ppermute x8 -> x0, starting transfers between devices: 15.4 us -> none  [the longest x4 12.8 us: with_halo(): lax.ppermute(lax.slice_in_dim(block, block.shape[dim] - width, None, axis...]
    gather x4 -> x0, local copies, waits for them, and re-layouts: 15.3 us -> none  [pick_cells(): return jnp.take(flat_rows, cell_ids, axis=1)]
  transfers between devices with their start and end apart: 9 -> 0, of which waited for: 4 -> 0; matrix products, arithmetic and copies ran while one was open for 27% -> 0% of each run, Pallas kernels for 0% -> 0%
where the time goes in v1:
time: 38.9 us; the launch traced here: 38.5 us
  Pallas kernels  29.8 us (77%)
  local copies, waits for them, and re-layouts  8.08 us (21%)
  between operations  0.69 us (2%)
    pallas_call x1, Pallas kernels, local(): pl.pallas_call(functools.partial(kernel, n_sector, n_axial, (modes, axial...  29.8 us
    unnamed x24, local copies, waits for them, and re-layouts  8.08 us

profile of v1, /device:TPU:1, one launch (start us, length us, event | category | flops | bytes accessed | tf_op | source)
XLA Modules:
  0.0 38.5 jit_solution(11364913917094116595)
XLA Ops:
  0.6 0.0 copy-start.7
  0.6 0.0 copy-start.6
  0.7 0.0 copy-start.5
  0.7 0.0 copy-start.4
  0.7 0.0 copy-start.10
  0.7 0.6 %copy-done.7 = s32[1,512]{1,0:T(1,128)S(1)} copy-done((s32[1,512]{1,0:T(1,128)S(1)}, s32[1,512]{1,0:T(1,128)}, u32[]{:S(2)}) %copy-start.7) | copy-done | bytes 2072
  1.3 0.0 copy-done.6
  1.3 0.0 copy-done.5
  1.3 0.0 copy-done.4
  1.4 0.0 copy-done.10
  1.4 0.0 copy-start
  1.4 1.2 %copy-done = f32[2,4,16,8,256]{4,3,2,1,0:T(8,128)S(1)} copy-done((f32[2,4,16,8,256]{4,3,2,1,0:T(8,128)S(1)}, f32[2,4,16,8,256]{4,3,2,1,0:T(8,128)}, u32[]{:S(2)}) %copy-start) | copy-done | bytes 1048600
  2.6 0.0 copy-start.1
  2.6 1.2 %copy-done.1 = f32[2,4,16,8,256]{4,3,2,1,0:T(8,128)S(1)} copy-done((f32[2,4,16,8,256]{4,3,2,1,0:T(8,128)S(1)}, f32[2,4,16,8,256]{4,3,2,1,0:T(8,128)}, u32[]{:S(2)}) %copy-start.1) | copy-done | bytes 1048600
  3.8 0.0 copy-start.2
  3.8 1.0 %copy-done.2 = bf16[2,4,16,8,256]{4,3,2,1,0:T(8,128)(2,1)S(1)} copy-done((bf16[2,4,16,8,256]{4,3,2,1,0:T(8,128)(2,1)S(1)}, bf16[2,4,16,8,256]{4,3,2,1,0:T(8,128)(2,1)}, u32[]{:S(2)}) %copy-start.2) | copy-done | bytes 524312
  4.9 0.0 copy-start.3
  4.9 0.9 %copy-done.3 = f32[16,8,256]{2,1,0:T(8,128)S(1)} copy-done((f32[16,8,256]{2,1,0:T(8,128)S(1)}, f32[16,8,256]{2,1,0:T(8,128)}, u32[]{:S(2)}) %copy-start.3) | copy-done | bytes 131096
  5.8 0.7 %copy-done.8 = s32[1,512,1]{1,2,0:T(1,128)S(1)} copy-done((s32[1,512,1]{1,2,0:T(1,128)S(1)}, s32[1,512,1]{1,2,0:T(1,128)}, u32[]{:S(2)}) %copy-start.8) | copy-done | bytes 2072
  6.5 0.0 copy-start.9
  6.5 0.7 %copy-done.9 = s32[1,512]{1,0:T(1,128)S(1)} copy-done((s32[1,512]{1,0:T(1,128)S(1)}, s32[1,512]{1,0:T(1,128)}, u32[]{:S(2)}) %copy-start.9) | copy-done | bytes 2072
  7.1 29.8 %helmholtz_steps.1 = (f32[8,128,256]{2,1,0:T(8,128)S(1)}, f32[128,256]{1,0:T(8,128)S(1)}) custom-call(f32[8,128,256]{2,1,0:T(8,128)S(1)} %bitcast.7, f32[8,128,256]{2,1,0:T(8,128)S(1)} %bitcast.8, f32[128,256]{1,0:T(8,128)S(1)} %bitcast.11, bf16[8,128,256]{2,1,0:T(8,128)(2,1)S(1)} %bitcast.10, f32[2,4]{1,0:T(2,128)S(1)} %copy-done.10, ...), custom_call_target="tpu_custom_call" | custom-call | tf_op jit(solution)/shard_map/helmholtz_steps/pallas_call | solution.py:602
  36.9 1.0 %copy.15 = f32[2,4,16,8,256]{4,3,2,1,0:T(8,128)} copy(f32[2,4,16,8,256]{4,3,2,1,0:T(8,128)S(1)} %bitcast.9) | data formatting | bytes 2097152
  37.9 0.7 %copy.16 = f32[16,8,256]{2,1,0:T(8,128)} copy(f32[16,8,256]{2,1,0:T(8,128)S(1)} %bitcast.12) | data formatting | bytes 262144
  (1 shorter events, 0.0 us)
Async XLA Ops:
  0.6 0.7 %copy-start.7 = (s32[1,512]{1,0:T(1,128)S(1)}, s32[1,512]{1,0:T(1,128)}, u32[]{:S(2)}) copy-start(s32[1,512]{1,0:T(1,128)} %source_hbm.1) | copy-start | bytes 6148
  0.6 0.7 %copy-start.6 = (s32[1,512]{1,0:T(1,128)S(1)}, s32[1,512]{1,0:T(1,128)}, u32[]{:S(2)}) copy-start(s32[1,512]{1,0:T(1,128)} %bin_hbm.1) | copy-start | bytes 6148
  0.7 0.7 %copy-start.5 = (f32[4,32]{1,0:T(4,128)S(1)}, f32[4,32]{1,0:T(4,128)}, u32[]{:S(2)}) copy-start(f32[4,32]{1,0:T(4,128)} %phase_hbm.1) | copy-start | bytes 1540
  0.7 0.7 %copy-start.4 = (f32[1,512]{1,0:T(1,128)S(1)}, f32[1,512]{1,0:T(1,128)}, u32[]{:S(2)}) copy-start(f32[1,512]{1,0:T(1,128)} %gain_hbm.1) | copy-start | bytes 6148
  0.7 0.7 %copy-start.10 = (f32[2,4]{1,0:T(2,128)S(1)}, f32[2,4]{1,0:T(2,128)}, u32[]{:S(2)}) copy-start(f32[2,4]{1,0:T(2,128)} %omega_hbm.1) | copy-start | bytes 100
  1.4 1.2 %copy-start = (f32[2,4,16,8,256]{4,3,2,1,0:T(8,128)S(1)}, f32[2,4,16,8,256]{4,3,2,1,0:T(8,128)}, u32[]{:S(2)}) copy-start(f32[2,4,16,8,256]{4,3,2,1,0:T(8,128)} %param.11) | copy-start | bytes 3145732
  2.6 1.2 %copy-start.1 = (f32[2,4,16,8,256]{4,3,2,1,0:T(8,128)S(1)}, f32[2,4,16,8,256]{4,3,2,1,0:T(8,128)}, u32[]{:S(2)}) copy-start(f32[2,4,16,8,256]{4,3,2,1,0:T(8,128)} %param.12) | copy-start | bytes 3145732
  3.8 1.0 %copy-start.2 = (bf16[2,4,16,8,256]{4,3,2,1,0:T(8,128)(2,1)S(1)}, bf16[2,4,16,8,256]{4,3,2,1,0:T(8,128)(2,1)}, u32[]{:S(2)}) copy-start(bf16[2,4,16,8,256]{4,3,2,1,0:T(8,128)(2,1)} %param.14) | copy-start | bytes 1572868
  4.9 0.9 %copy-start.3 = (f32[16,8,256]{2,1,0:T(8,128)S(1)}, f32[16,8,256]{2,1,0:T(8,128)}, u32[]{:S(2)}) copy-start(f32[16,8,256]{2,1,0:T(8,128)} %param.13) | copy-start | bytes 393220
  5.8 0.7 %copy-start.8 = (s32[1,512,1]{1,2,0:T(1,128)S(1)}, s32[1,512,1]{1,2,0:T(1,128)}, u32[]{:S(2)}) copy-start(s32[1,512,1]{1,2,0:T(1,128)} %param.20) | copy-start | bytes 6148
  6.5 0.7 %copy-start.9 = (s32[1,512]{1,0:T(1,128)S(1)}, s32[1,512]{1,0:T(1,128)}, u32[]{:S(2)}) copy-start(s32[1,512]{1,0:T(1,128)} %target_hbm.1) | copy-start | bytes 6148

commit v2 on v1

v2 whole, which is shorter than its diff:
```python
import functools

import jax
import jax.numpy as jnp
from jax import lax
from jax.experimental import pallas as pl
from jax.experimental.pallas import tpu as pltpu
from jax.sharding import PartitionSpec as P

ITERS = 2
RELAX = 0.6
CAP = 96
LANES = 128
MESH = pl.DeviceIdType.MESH
BF16 = jnp.bfloat16
F32 = jnp.float32
I32 = jnp.int32


def one_hot(flags):
    return jnp.where(flags, 1.0, 0.0).astype(BF16)


def halves(values):
    high = values.astype(BF16)
    return high, (values - high.astype(F32)).astype(BF16)


def dot_nt(left, right):
    return lax.dot_general(
        left, right, (((1,), (1,)), ((), ())), preferred_element_type=F32
    )


def read(ref, *index):
    *lead, at = index
    tiles = ref.shape[len(lead)]
    return jnp.concatenate([ref[(*lead, i, at)] for i in range(tiles)], axis=-1)


def write(ref, *index_and_value):
    *lead, at, value = index_and_value
    for i in range(ref.shape[len(lead)]):
        ref[(*lead, i, at)] = value[..., i * LANES : (i + 1) * LANES]


def flip(sector, mask, n_sector):
    bit = 1
    other = sector
    while bit < n_sector:
        if mask & bit:
            other = other + bit * (1 - 2 * (sector // bit % 2))
        bit *= 2
    return other


def partner_order(n_sector):
    hops = {mask: (0, 1, 2, 1)[mask // 2 % 4] + mask // 8 for mask in range(n_sector)}
    return sorted(range(n_sector), key=lambda mask: (hops[mask], mask))


def kernel(
    n_sector,
    n_axial,
    shape,
    rhs_hbm,
    start_hbm,
    sound_hbm,
    direct_hbm,
    omega_hbm,
    gain_hbm,
    phase_hbm,
    bin_hbm,
    source_hbm,
    sector_hbm,
    target_hbm,
    adjoint,
    sensitivity,
    rhs,
    field_a,
    field_b,
    sound,
    direct,
    omega,
    gain,
    phase,
    bins,
    source,
    sector,
    target,
    base,
    scale,
    k_axial,
    k_rest,
    edge,
    pick_radial,
    pick_row,
    picked_start,
    lane_hot,
    block_hot,
    gain_cos,
    gain_sin,
    put_row,
    put_edge,
    put_radial,
    match,
    sound_send,
    sound_side,
    side_send,
    side_recv,
    end_send,
    cell_send,
    cell_recv,
    flame_send,
    flame_recv,
    sens_own,
    sens_other,
    in_sem,
    sound_sems,
    halo_sems,
    cell_sems,
    flame_sems,
    sens_sems,
):
    modes, axial_cells, azimuth_cells, radial_cells = shape
    channels = 2 * modes
    rows = axial_cells * azimuth_cells
    flames = gain.shape[1]
    tiles = radial_cells // LANES
    half_blocks = n_sector // 2
    half = half_blocks * CAP
    near, far = 0, 1
    axial = lax.axis_index("axial")
    my_sector = lax.axis_index("sector")
    my_modes = lax.axis_index("modes")
    up_axial = lax.rem(axial + 1, n_axial)
    down_axial = lax.rem(axial + n_axial - 1, n_axial)
    next_sector = lax.rem(my_sector + 1, n_sector)
    last_sector = lax.rem(my_sector + n_sector - 1, n_sector)
    partners = [flip(my_sector, mask, n_sector) for mask in partner_order(n_sector)]

    barrier = pltpu.get_barrier_semaphore()
    for other in partners[1:]:
        pl.semaphore_signal(barrier, inc=1, device_id={"sector": other}, device_id_type=MESH)
    for other in (next_sector, last_sector):
        pl.semaphore_signal(barrier, inc=1, device_id={"sector": other}, device_id_type=MESH)
    for other in (up_axial, down_axial):
        pl.semaphore_signal(barrier, inc=1, device_id={"axial": other}, device_id_type=MESH)
    pl.semaphore_signal(
        barrier, inc=1, device_id={"modes": 1 - my_modes}, device_id_type=MESH
    )

    inner = pl.ds(azimuth_cells, rows)
    pieces = [pl.ds(i * LANES, LANES) for i in range(tiles)]
    loads = {}
    for name, source_ref, target_ref in (
        [("sector", sector_hbm, sector), ("target", target_hbm, target), ("source", source_hbm, source)]
        + [(("start", i), start_hbm.at[:, :, pieces[i]], field_a.at[:, i, inner]) for i in range(tiles)]
        + [(("sound", i), sound_hbm.at[:, pieces[i]], sound.at[i, inner]) for i in range(tiles)]
        + [("bins", bin_hbm, bins), ("phase", phase_hbm, phase), ("gain", gain_hbm, gain)]
        + [("omega", omega_hbm, omega), ("rhs", rhs_hbm, rhs), ("direct", direct_hbm, direct)]
    ):
        loads[name] = pltpu.make_async_copy(source_ref, target_ref, in_sem.at[len(loads)])
        if name not in ("rhs", "direct"):
            loads[name].start()

    def loaded(*names):
        for name in names:
            loads[name].wait()

    loaded("sector", "target", "source")
    partner = jnp.zeros((n_sector, LANES), I32)
    position = lax.broadcasted_iota(I32, (n_sector, LANES), 0)
    for p, other in enumerate(partners):
        partner = jnp.where(position == p, other, partner)
    partner = jnp.concatenate([partner] * (flames // LANES), axis=1)
    in_block = jnp.where(jnp.broadcast_to(sector[...], (n_sector, flames)) == partner, 1.0, 0.0)
    block_hot[...] = in_block
    before = one_hot(
        lax.broadcasted_iota(I32, (flames, flames), 0)
        < lax.broadcasted_iota(I32, (flames, flames), 1)
    )
    earlier = jnp.dot(in_block.astype(BF16), before, preferred_element_type=F32)
    rank = jnp.sum(in_block * earlier, axis=0, keepdims=True).astype(I32)
    block_of = jnp.sum(
        in_block * lax.broadcasted_iota(I32, (n_sector, flames), 0).astype(F32),
        axis=0,
        keepdims=True,
    ).astype(I32)
    lane = (rank + CAP * block_of) & (LANES - 1)
    lane_hot[...] = one_hot(
        lax.broadcasted_iota(I32, (LANES, flames), 0) == jnp.broadcast_to(lane, (LANES, flames))
    )

    def pack(parts):
        left = jnp.concatenate(
            [
                jnp.concatenate(
                    [part * block_hot[p : p + 1, :] for p in range(n_sector)], axis=0
                ).astype(BF16)
                for part in parts
            ],
            axis=0,
        )
        packed = dot_nt(left, lane_hot[...])
        total = packed[: 8 * n_sector]
        for i in range(1, len(parts)):
            total = total + packed[8 * n_sector * i : 8 * n_sector * (i + 1)]
        return total.reshape(n_sector, 8, LANES)

    target_row = (target[...] // radial_cells).astype(F32)
    target_radial = (target[...] % radial_cells).astype(F32)
    sub = lax.broadcasted_iota(I32, (8, flames), 0)
    cell_send[...] = pack(
        [
            jnp.where(
                sub == 0,
                jnp.broadcast_to(target_row, (8, flames)),
                jnp.where(sub == 1, jnp.broadcast_to(target_radial, (8, flames)), 0.0),
            )
        ]
    )

    def remote(src, dst, sems, i, device):
        return pltpu.make_async_remote_copy(
            src_ref=src,
            dst_ref=dst,
            send_sem=sems.at[0, i],
            recv_sem=sems.at[1, i],
            device_id=device,
            device_id_type=MESH,
        )

    low_pad = pl.ds(0, azimuth_cells)
    high_pad = pl.ds(rows + azimuth_cells, azimuth_cells)
    first_rows = pl.ds(azimuth_cells, azimuth_cells)
    last_rows = pl.ds(rows, azimuth_cells)

    def side_halo(send, recv, sems):
        return [
            remote(send.at[1], recv.at[0], sems, 2, {"sector": next_sector}),
            remote(send.at[0], recv.at[1], sems, 3, {"sector": last_sector}),
        ]

    def blocks(send, recv, sems):
        return [
            remote(send.at[p], recv.at[p], sems, p, {"sector": partners[p]})
            for p in reversed(range(1, n_sector))
        ]

    sends = []

    def start(copies):
        for copy in copies:
            copy.start()
        sends.extend(copies)
        return copies

    def received(copies):
        for copy in copies:
            copy.wait_recv()

    side_rows = [
        pl.ds(row, axial_cells, azimuth_cells) for row in (0, azimuth_cells - 1)
    ]
    padded_side_rows = [
        pl.ds(azimuth_cells + row, axial_cells, azimuth_cells) for row in (0, azimuth_cells - 1)
    ]

    loaded(*[("sound", i) for i in range(tiles)])
    for side in range(2):
        for i in range(tiles):
            sound_send[side, i] = sound[i, padded_side_rows[side], :]
    loaded(*[("start", i) for i in range(tiles)])
    loads["rhs"].start()
    for side in range(2):
        for c in range(channels):
            for i in range(tiles):
                side_send[0, side, c, i] = field_a[c, i, padded_side_rows[side], :]

    pl.semaphore_wait(barrier, n_sector + 4)

    cell_copies = start(blocks(cell_send, cell_recv, cell_sems))
    sound_copies = start(
        [
            remote(sound.at[:, last_rows], sound.at[:, low_pad], sound_sems, 0, {"axial": up_axial}),
            remote(sound.at[:, first_rows], sound.at[:, high_pad], sound_sems, 1, {"axial": down_axial}),
        ]
        + side_halo(sound_send, sound_side, sound_sems)
    )
    cell_recv[0] = cell_send[0]
    sems = halo_sems.at[0]
    halo_copies = start(
        side_halo(side_send.at[0], side_recv.at[0], sems)
        + [
            remote(field_a.at[:, :, last_rows], field_a.at[:, :, low_pad], sems, 0, {"axial": up_axial}),
            remote(field_a.at[:, :, first_rows], field_a.at[:, :, high_pad], sems, 1, {"axial": down_axial}),
        ]
    )

    cell = source[...]
    row_of = jnp.broadcast_to(cell // radial_cells, (rows, flames))
    pick_row[...] = jnp.where(lax.broadcasted_iota(I32, (rows, flames), 0) == row_of, 1.0, 0.0)
    radial_of = jnp.broadcast_to(cell % radial_cells, (radial_cells, flames))
    radial_hot = one_hot(lax.broadcasted_iota(I32, (radial_cells, flames), 0) == radial_of)
    pick_radial[:radial_cells] = radial_hot
    pick_radial[radial_cells:] = radial_hot

    loaded("bins", "phase", "gain")
    bin_count = phase.shape[1]
    bin_hot = jnp.where(
        lax.broadcasted_iota(I32, (bin_count, flames), 0)
        == jnp.broadcast_to(bins[...], (bin_count, flames)),
        1.0,
        0.0,
    )
    angle = phase[...]
    gains = jnp.broadcast_to(gain[...], (modes, flames))
    exact = lax.Precision.HIGHEST
    gain_cos[...] = gains * jnp.dot(
        jnp.cos(angle), bin_hot, precision=exact, preferred_element_type=F32
    )
    gain_sin[...] = -gains * jnp.dot(
        jnp.sin(angle), bin_hot, precision=exact, preferred_element_type=F32
    )

    def pick(planes):
        high, low = halves(jnp.concatenate(planes, axis=0))
        columns = jnp.dot(
            jnp.concatenate([high, low], axis=1), pick_radial[...], preferred_element_type=F32
        ).reshape(len(planes), rows, flames)
        return jnp.sum(columns * pick_row[...][None], axis=1)

    def pick_field(ref, at):
        return jnp.concatenate(
            [
                pick([read(ref, g * modes + m, at) for m in range(modes)])
                for g in range(2)
            ],
            axis=0,
        )

    def send_flames(picked, step):
        real, imag = picked[:modes], picked[modes:]
        cosines, sines = gain_cos[...], gain_sin[...]
        amounts = jnp.concatenate(
            [cosines * real - sines * imag, cosines * imag + sines * real], axis=0
        )
        high = amounts.astype(BF16).astype(F32)
        flame_send[step] = pack([high, amounts - high])
        copies = start(blocks(flame_send.at[step], flame_recv.at[step], flame_sems.at[step]))
        flame_recv[step, 0] = flame_send[step, 0]
        return copies[half_blocks:], copies[:half_blocks]

    picked_start[...] = pick_field(field_a, inner)
    near_copies, far_copies = send_flames(picked_start[...], 0)

    tile = (azimuth_cells, radial_cells)
    azimuth = lax.broadcasted_iota(I32, tile, 0)
    radial = lax.broadcasted_iota(I32, tile, 1)

    def own_rows(a):
        return pl.ds(pl.multiple_of(a * azimuth_cells, azimuth_cells), azimuth_cells)

    def couplings(a, _):
        s = read(sound, own_rows(a + 1))
        at = own_rows(a)
        k_rest[0, at, :] = jnp.where(azimuth == 0, 0.0, 0.5 * (s + pltpu.roll(s, 1, 0)))
        k_rest[1, at, :] = jnp.where(
            azimuth == azimuth_cells - 1, 0.0, 0.5 * (s + pltpu.roll(s, azimuth_cells - 1, 0))
        )
        k_rest[2, at, :] = jnp.where(radial == 0, 0.0, 0.5 * (s + pltpu.roll(s, 1, 1)))
        k_rest[3, at, :] = jnp.where(
            radial == radial_cells - 1, 0.0, 0.5 * (s + pltpu.roll(s, radial_cells - 1, 1))
        )
        return 0

    def axial_coupling(a, _):
        k_axial[own_rows(a), :] = 0.5 * (read(sound, own_rows(a)) + read(sound, own_rows(a + 1)))
        return 0

    lax.fori_loop(0, axial_cells, couplings, 0)
    lax.fori_loop(1, axial_cells, axial_coupling, 0)

    loaded("omega", "rhs")
    loads["direct"].start()
    omega_real = [omega[0, m] for m in range(modes)]
    omega_imag = [omega[1, m] for m in range(modes)]

    def base_rows(field, a, low, high):
        at, mid, top = own_rows(a), own_rows(a + 1), own_rows(a + 2)
        k_slo, k_shi, k_rlo, k_rhi = (k_rest[i, at, :] for i in range(4))
        k_alo = k_axial[at, :] if low else None
        k_ahi = k_axial[mid, :] if high else None
        for m in range(modes):
            real, imag = read(field, m, mid), read(field, modes + m, mid)
            for c, x, mass in (
                (m, real, omega_real[m] * real - omega_imag[m] * imag),
                (modes + m, imag, omega_real[m] * imag + omega_imag[m] * real),
            ):
                total = rhs[c, at, :] + mass
                if low:
                    total = total + k_alo * read(field, c, at)
                if high:
                    total = total + k_ahi * read(field, c, top)
                total = total + k_slo * pltpu.roll(x, 1, 0)
                total = total + k_shi * pltpu.roll(x, azimuth_cells - 1, 0)
                total = total + k_rlo * pltpu.roll(x, 1, 1)
                total = total + k_rhi * pltpu.roll(x, radial_cells - 1, 1)
                write(base, c, at, total)

    def make_base(field):
        lax.fori_loop(
            1, axial_cells - 1, lambda a, _: (base_rows(field, a, True, True), 0)[1], 0
        )
        base_rows(field, 0, False, True)
        base_rows(field, axial_cells - 1, True, False)

    first_axial = axial == 0
    last_axial = axial == n_axial - 1
    first, last = pl.ds(0, azimuth_cells), pl.ds(rows - azimuth_cells, azimuth_cells)

    def add_halo(field, step):
        k_low = k_axial[pl.ds(0, azimuth_cells), :]
        k_high = k_axial[pl.ds(rows, azimuth_cells), :]
        for c in range(channels):
            below = jnp.where(first_axial, 0.0, read(field, c, low_pad))
            write(base, c, first, read(base, c, first) + k_low * below)
            above = jnp.where(last_axial, 0.0, read(field, c, high_pad))
            write(base, c, last, read(base, c, last) + k_high * above)
        for side in range(2):
            at = side_rows[side]
            for c in range(channels):
                for i in range(tiles):
                    base[c, i, at, :] = (
                        base[c, i, at, :] + edge[side, i] * side_recv[step, side, c, i]
                    )

    make_base(field_a)

    def squeeze(recv, group):
        lanes = lax.broadcasted_iota(I32, (8, LANES), 1)
        parts = []
        for start_block in range(group * half_blocks, (group + 1) * half_blocks, 4):
            b = [recv[start_block + i] for i in range(4)]
            parts.append(jnp.where(lanes < 96, b[0], b[1]))
            parts.append(jnp.where(lanes < 64, b[1], b[2]))
            parts.append(jnp.where(lanes < 32, b[2], b[3]))
        return jnp.concatenate(parts, axis=1)

    def put_hots(group):
        cells = squeeze(cell_recv, group)
        row, column = cells[0:1], cells[1:2]
        put_row[group] = one_hot(
            lax.broadcasted_iota(I32, (rows, half), 0).astype(F32)
            == jnp.broadcast_to(row, (rows, half))
        )
        upright = jnp.broadcast_to(column, (LANES, half)).T
        put_radial[group] = one_hot(
            jnp.concatenate([upright] * tiles, axis=1)
            == lax.broadcasted_iota(I32, (half, radial_cells), 1).astype(F32)
        )
        return row, column

    def add_flames(parts, hot, group):
        left = jnp.concatenate(
            [hot * part[c : c + 1, :] for part in parts for c in range(channels)], axis=0
        )
        totals = jnp.dot(left, put_radial[group], preferred_element_type=F32)
        middle = totals.shape[0] // 2
        return totals[:middle] + totals[middle:]

    chunk = rows // 4

    def subtract_near(step):
        parts = halves(squeeze(flame_recv.at[step], near))
        for top in range(0, rows, chunk):
            at = pl.ds(top, chunk)
            totals = add_flames(parts, put_row[near, top : top + chunk, :], near)
            for c in range(channels):
                write(base, c, at, read(base, c, at) - totals[c * chunk : (c + 1) * chunk])

    received(cell_copies[half_blocks:])
    put_hots(near)
    received(near_copies)
    subtract_near(0)

    received(sound_copies)
    k_axial[first, :] = 0.5 * (
        read(sound, first_rows) + jnp.where(first_axial, 0.0, read(sound, low_pad))
    )
    k_axial[pl.ds(rows, azimuth_cells), :] = 0.5 * (
        read(sound, last_rows) + jnp.where(last_axial, 0.0, read(sound, high_pad))
    )
    for side in range(2):
        for i in range(tiles):
            edge[side, i] = 0.5 * (sound[i, padded_side_rows[side], :] + sound_side[side, i])

    def scales(a, _):
        at = own_rows(a)
        low = jnp.broadcast_to(read(edge, 0, pl.ds(a, 1)), tile)
        high = jnp.broadcast_to(read(edge, 1, pl.ds(a, 1)), tile)
        weights = k_axial[at, :] + k_axial[own_rows(a + 1), :] + k_rest[2, at, :] + k_rest[3, at, :]
        weights = weights + jnp.where(azimuth == 0, low, k_rest[0, at, :])
        weights = weights + jnp.where(azimuth == azimuth_cells - 1, high, k_rest[1, at, :])
        write(scale, at, RELAX / weights)
        return 0

    lax.fori_loop(0, axial_cells, scales, 0)
    all_rows = pl.ds(0, rows)
    picked_scale = pick([read(scale, all_rows)])

    received(cell_copies[:half_blocks])
    row, column = put_hots(far)
    edge_rows = 2 * axial_cells + 2 * azimuth_cells
    i = lax.broadcasted_iota(I32, (edge_rows, half), 0)
    edge_row = jnp.where(
        i < axial_cells,
        i * azimuth_cells,
        jnp.where(
            i < 2 * axial_cells,
            (i - axial_cells) * azimuth_cells + azimuth_cells - 1,
            jnp.where(
                i < 2 * axial_cells + azimuth_cells,
                i - 2 * axial_cells,
                i - 2 * axial_cells - 2 * azimuth_cells + rows,
            ),
        ),
    )
    put_edge[...] = one_hot(edge_row.astype(F32) == jnp.broadcast_to(row, (edge_rows, half)))
    upright = jnp.broadcast_to(row * radial_cells + column, (LANES, half)).T
    match[...] = one_hot(
        jnp.concatenate([upright] * (flames // LANES), axis=1)
        == jnp.broadcast_to(cell.astype(F32), (half, flames))
    )

    received(halo_copies)
    add_halo(field_a, 0)
    picked_base = pick_field(base, all_rows)

    received(far_copies)
    parts = halves(squeeze(flame_recv.at[0], far))
    found = jnp.dot(jnp.concatenate(parts, axis=0), match[...], preferred_element_type=F32)
    found = found[:channels] + found[channels:]
    picked = (1.0 - RELAX) * picked_start[...] + picked_scale * (picked_base - found)
    near_copies, far_copies = send_flames(picked, 1)

    totals = add_flames(parts, put_edge[...], far)
    for c in range(channels):
        here = c * edge_rows
        for side in range(2):
            for i in range(tiles):
                added = totals[
                    here + side * axial_cells : here + (side + 1) * axial_cells,
                    i * LANES : (i + 1) * LANES,
                ]
                side_send[1, side, c, i] = (1.0 - RELAX) * side_send[0, side, c, i] + scale[
                    i, side_rows[side], :
                ] * (base[c, i, side_rows[side], :] - added)
        here = here + 2 * axial_cells
        for end, at, padded_at in ((0, first, first_rows), (1, last, last_rows)):
            added = totals[here + end * azimuth_cells : here + (end + 1) * azimuth_cells]
            write(
                end_send,
                end,
                c,
                pl.ds(0, azimuth_cells),
                (1.0 - RELAX) * read(field_a, c, padded_at)
                + read(scale, at) * (read(base, c, at) - added),
            )
    sems = halo_sems.at[1]
    halo_copies = start(
        side_halo(side_send.at[1], side_recv.at[1], sems)
        + [
            remote(end_send.at[1], field_b.at[:, :, low_pad], sems, 0, {"axial": up_axial}),
            remote(end_send.at[0], field_b.at[:, :, high_pad], sems, 1, {"axial": down_axial}),
        ]
    )

    for top in range(0, rows, chunk):
        totals = add_flames(parts, put_row[far, top : top + chunk, :], far)
        at = pl.ds(top, chunk)
        padded_at = pl.ds(top + azimuth_cells, chunk)
        for c in range(channels):
            write(
                field_b,
                c,
                padded_at,
                (1.0 - RELAX) * read(field_a, c, padded_at)
                + read(scale, at) * (read(base, c, at) - totals[c * chunk : (c + 1) * chunk]),
            )

    make_base(field_b)
    received(near_copies)
    subtract_near(1)
    received(halo_copies)
    add_halo(field_b, 1)
    loaded("direct")
    received(far_copies)
    parts = halves(squeeze(flame_recv.at[1], far))
    sens_copies = []
    for number, top in enumerate(range(0, rows, chunk)):
        totals = add_flames(parts, put_row[far, top : top + chunk, :], far)
        at = pl.ds(top, chunk)
        padded_at = pl.ds(top + azimuth_cells, chunk)
        sens = jnp.zeros((chunk, radial_cells), F32)
        for c in range(channels):
            x = (1.0 - RELAX) * read(field_b, c, padded_at) + read(scale, at) * (
                read(base, c, at) - totals[c * chunk : (c + 1) * chunk]
            )
            adjoint[c, at, :] = x
            term = x * direct[c, at, :].astype(F32)
            sens = sens + term if c < modes else sens - term
        sens_own[at, :] = sens
        sens_copies += start(
            [remote(sens_own.at[at], sens_other.at[at], sens_sems, number, {"modes": 1 - my_modes})]
        )
    for number, top in enumerate(range(0, rows, chunk)):
        at = pl.ds(top, chunk)
        received([sens_copies[number]])
        sensitivity[at, :] = sens_own[at, :] + sens_other[at, :]
    for copy in sends:
        copy.wait_send()


def local(
    n_sector,
    n_axial,
    rhs,
    adjoint_start,
    sound_sq,
    direct_mode,
    omega_sq,
    flame_gain,
    delay_phase,
    delay_bin,
    flame_cell,
    injector_sector,
    injector_cell,
):
    parts, modes, axial_cells, azimuth_cells, radial_cells = rhs.shape
    channels = parts * modes
    rows = axial_cells * azimuth_cells
    flames = flame_cell.shape[1]
    half = n_sector // 2 * CAP
    tiles = radial_cells // LANES
    block = (channels, rows, radial_cells)
    padded = (channels, tiles, rows + 2 * azimuth_cells, LANES)
    side = (tiles, axial_cells, LANES)
    plane = (rows, radial_cells)
    dma = pltpu.SemaphoreType.DMA
    vmem = pltpu.VMEM
    scratch = [
        vmem(block, F32),
        vmem(padded, F32),
        vmem(padded, F32),
        vmem(padded[1:], F32),
        vmem(block, BF16),
        pltpu.SMEM((2, modes), F32),
        vmem((1, flames), F32),
        vmem(delay_phase.shape, F32),
        vmem((1, flames), I32),
        vmem((1, flames), I32),
        vmem((1, flames), I32),
        vmem((1, flames), I32),
        vmem((channels, tiles, rows, LANES), F32),
        vmem((tiles, rows, LANES), F32),
        vmem((rows + azimuth_cells, radial_cells), F32),
        vmem((4,) + plane, F32),
        vmem((2,) + side, F32),
        vmem((2 * radial_cells, flames), BF16),
        vmem((rows, flames), F32),
        vmem((channels, flames), F32),
        vmem((LANES, flames), BF16),
        vmem((n_sector, flames), F32),
        vmem((modes, flames), F32),
        vmem((modes, flames), F32),
        vmem((2, rows, half), BF16),
        vmem((2 * (axial_cells + azimuth_cells), half), BF16),
        vmem((2, half, radial_cells), BF16),
        vmem((half, flames), BF16),
        vmem((2,) + side, F32),
        vmem((2,) + side, F32),
        vmem((ITERS, 2, channels) + side, F32),
        vmem((ITERS, 2, channels) + side, F32),
        vmem((2, channels, tiles, azimuth_cells, LANES), F32),
        vmem((n_sector, 8, LANES), F32),
        vmem((n_sector, 8, LANES), F32),
        vmem((ITERS, n_sector, 8, LANES), F32),
        vmem((ITERS, n_sector, 8, LANES), F32),
        vmem(plane, F32),
        vmem(plane, F32),
        dma((9 + 2 * tiles,)),
        dma((2, 4)),
        dma((ITERS, 2, 4)),
        dma((2, n_sector)),
        dma((ITERS, 2, n_sector)),
        dma((2, 4)),
    ]
    in_hbm = pl.BlockSpec(memory_space=pltpu.HBM)

    def stay(array):
        return pltpu.with_memory_space_constraint(array, pltpu.HBM)

    in_vmem = pl.BlockSpec(memory_space=pltpu.VMEM)
    adjoint, sensitivity = pl.pallas_call(
        functools.partial(
            kernel, n_sector, n_axial, (modes, axial_cells, azimuth_cells, radial_cells)
        ),
        out_shape=(jax.ShapeDtypeStruct(block, F32), jax.ShapeDtypeStruct(plane, F32)),
        in_specs=[in_hbm] * 11,
        out_specs=(in_vmem, in_vmem),
        scratch_shapes=scratch,
        compiler_params=pltpu.CompilerParams(
            collective_id=0, has_side_effects=True, vmem_limit_bytes=40 * 1024 * 1024
        ),
        name="helmholtz_steps",
    )(
        stay(rhs.reshape(block)),
        stay(adjoint_start.reshape(block)),
        stay(sound_sq.reshape(plane)),
        stay(direct_mode.reshape(block)),
        stay(omega_sq),
        stay(flame_gain),
        stay(delay_phase),
        stay(delay_bin),
        stay(flame_cell),
        stay(injector_sector.reshape(1, flames)),
        stay(injector_cell),
    )
    return adjoint.reshape(rhs.shape), sensitivity.reshape(sound_sq.shape)


def solution(mesh):
    placed = (
        P(None, "modes", "axial", "sector", None),
        P(None, "modes", "axial", "sector", None),
        P("axial", "sector", None),
        P(None, "modes", "axial", "sector", None),
        P(None, "modes"),
        P("axial", "sector"),
        P("modes", None),
        P("axial", "sector"),
        P("axial", "sector"),
        P("axial", "sector", None),
        P("axial", "sector"),
    )
    return jax.shard_map(
        functools.partial(local, mesh.shape["sector"], mesh.shape["axial"]),
        mesh=mesh,
        in_specs=placed,
        out_specs=(P(None, "modes", "axial", "sector", None), P("axial", "sector", None)),
        check_vma=False,
    )
```

time: 38.9 us -> 31.1 us (0.80)
  local copies, waits for them, and re-layouts: 8.08 us -> 1.63 us
  Pallas kernels: 29.8 us -> 28.7 us
    unnamed x24 -> x2, local copies, waits for them, and re-layouts: 8.08 us -> 1.63 us
    pallas_call x1, Pallas kernels: 29.8 us -> 28.7 us  [local(): pl.pallas_call(functools.partial(kernel, n_sector, n_axial, (modes, axial...]
where the time goes in v2:
time: 31.1 us; the launch traced here: 31 us
  Pallas kernels  28.7 us (92%)
  local copies, waits for them, and re-layouts  1.63 us (5%)
  between operations  0.64 us (2%)
    pallas_call x1, Pallas kernels, local(): pl.pallas_call(functools.partial(kernel, n_sector, n_axial, (modes, axial...  28.7 us
    unnamed x2, local copies, waits for them, and re-layouts  1.63 us

profile of v2, /device:TPU:1, one launch (start us, length us, event | category | flops | bytes accessed | tf_op | source)
XLA Modules:
  0.0 31.0 jit_solution(241075450075254394)
XLA Ops:
  0.6 28.7 %helmholtz_steps.1 = (f32[8,128,256]{2,1,0:T(8,128)S(1)}, f32[128,256]{1,0:T(8,128)S(1)}) custom-call(f32[8,128,256]{2,1,0:T(8,128)} %bitcast.9, f32[8,128,256]{2,1,0:T(8,128)} %bitcast.10, f32[128,256]{1,0:T(8,128)} %bitcast.12, bf16[8,128,256]{2,1,0:T(8,128)(2,1)} %bitcast.11, f32[2,4]{1,0:T(2,128)} %omega_hbm.1, f32[1,512]{1,0:T(1,128)} %gain_hbm.1, ...), custom_call_target="tpu_custom_call" | custom-call | tf_op jit(solution)/shard_map/helmholtz_steps/pallas_call | solution.py:706
  29.4 1.0 %copy.15 = f32[2,4,16,8,256]{4,3,2,1,0:T(8,128)} copy(f32[2,4,16,8,256]{4,3,2,1,0:T(8,128)S(1)} %bitcast.7) | data formatting | bytes 2097152
  30.3 0.7 %copy.16 = f32[16,8,256]{2,1,0:T(8,128)} copy(f32[16,8,256]{2,1,0:T(8,128)S(1)} %bitcast.8) | data formatting | bytes 262144

commit v3 on v2

--- a/solution.py
+++ b/solution.py
@@ -109,12 +109,21 @@
     side_send,
     side_recv,
     end_send,
+    end_recv,
+    sound_end,
     cell_send,
     cell_recv,
     flame_send,
     flame_recv,
+    direct_tiles,
+    slot_direct,
     sens_own,
     sens_other,
+    sens_sum,
+    edge_own,
+    edge_other,
+    slot_own,
+    slot_other,
     in_sem,
     sound_sems,
     halo_sems,
@@ -155,9 +164,9 @@
     loads = {}
     for name, source_ref, target_ref in (
         [("sector", sector_hbm, sector), ("target", target_hbm, target), ("source", source_hbm, source)]
+        + [("bins", bin_hbm, bins), ("phase", phase_hbm, phase), ("gain", gain_hbm, gain)]
+        + [(("sound", i), sound_hbm.at[:, pieces[i]], sound.at[i, inner]) for i in range(tiles)]
         + [(("start", i), start_hbm.at[:, :, pieces[i]], field_a.at[:, i, inner]) for i in range(tiles)]
-        + [(("sound", i), sound_hbm.at[:, pieces[i]], sound.at[i, inner]) for i in range(tiles)]
-        + [("bins", bin_hbm, bins), ("phase", phase_hbm, phase), ("gain", gain_hbm, gain)]
         + [("omega", omega_hbm, omega), ("rhs", rhs_hbm, rhs), ("direct", direct_hbm, direct)]
     ):
         loads[name] = pltpu.make_async_copy(source_ref, target_ref, in_sem.at[len(loads)])
@@ -221,44 +230,50 @@
         ]
     )
 
-    def remote(src, dst, sems, i, device):
+    def remote(src, dst, send_sem, recv_sem, device):
         return pltpu.make_async_remote_copy(
             src_ref=src,
             dst_ref=dst,
-            send_sem=sems.at[0, i],
-            recv_sem=sems.at[1, i],
+            send_sem=send_sem,
+            recv_sem=recv_sem,
             device_id=device,
             device_id_type=MESH,
         )
 
-    low_pad = pl.ds(0, azimuth_cells)
-    high_pad = pl.ds(rows + azimuth_cells, azimuth_cells)
+    def wait_bytes(ref, sem):
+        pltpu.make_async_copy(ref, ref, sem).wait()
+
     first_rows = pl.ds(azimuth_cells, azimuth_cells)
     last_rows = pl.ds(rows, azimuth_cells)
-
-    def side_halo(send, recv, sems):
-        return [
-            remote(send.at[1], recv.at[0], sems, 2, {"sector": next_sector}),
-            remote(send.at[0], recv.at[1], sems, 3, {"sector": last_sector}),
-        ]
-
-    def blocks(send, recv, sems):
-        return [
-            remote(send.at[p], recv.at[p], sems, p, {"sector": partners[p]})
-            for p in reversed(range(1, n_sector))
-        ]
-
-    sends = []
-
-    def start(copies):
-        for copy in copies:
-            copy.start()
-        sends.extend(copies)
-        return copies
-
-    def received(copies):
-        for copy in copies:
-            copy.wait_recv()
+    sent = []
+
+    def start_sides(send, recv, sems):
+        remote(send.at[1], recv.at[0], sems.at[0, 0], sems.at[1, 0], {"sector": next_sector}).start()
+        remote(send.at[0], recv.at[1], sems.at[0, 0], sems.at[1, 0], {"sector": last_sector}).start()
+        sent.append((recv, sems.at[0, 0]))
+
+    def start_ends(first, last, recv, sems):
+        remote(last, recv.at[0], sems.at[0, 1], sems.at[1, 1], {"axial": up_axial}).start()
+        remote(first, recv.at[1], sems.at[0, 1], sems.at[1, 1], {"axial": down_axial}).start()
+        sent.append((recv, sems.at[0, 1]))
+
+    def start_blocks(send, recv, sems):
+        for p in reversed(range(1, n_sector)):
+            group = 0 if p < half_blocks else 1
+            remote(
+                send.at[p], recv.at[p], sems.at[2], sems.at[group], {"sector": partners[p]}
+            ).start()
+        sent.append((send.at[pl.ds(1, n_sector - 1)], sems.at[2]))
+
+    def wait_blocks(recv, sems, group):
+        start = max(1, group * half_blocks)
+        wait_bytes(recv.at[pl.ds(start, (group + 1) * half_blocks - start)], sems.at[group])
+
+    def start_partner(send, recv, i):
+        remote(
+            send, recv, sens_sems.at[0, i], sens_sems.at[1, i], {"modes": 1 - my_modes}
+        ).start()
+        sent.append((send, sens_sems.at[0, i]))
 
     side_rows = [
         pl.ds(row, axial_cells, azimuth_cells) for row in (0, azimuth_cells - 1)
@@ -266,37 +281,6 @@
     padded_side_rows = [
         pl.ds(azimuth_cells + row, axial_cells, azimuth_cells) for row in (0, azimuth_cells - 1)
     ]
-
-    loaded(*[("sound", i) for i in range(tiles)])
-    for side in range(2):
-        for i in range(tiles):
-            sound_send[side, i] = sound[i, padded_side_rows[side], :]
-    loaded(*[("start", i) for i in range(tiles)])
-    loads["rhs"].start()
-    for side in range(2):
-        for c in range(channels):
-            for i in range(tiles):
-                side_send[0, side, c, i] = field_a[c, i, padded_side_rows[side], :]
-
-    pl.semaphore_wait(barrier, n_sector + 4)
-
-    cell_copies = start(blocks(cell_send, cell_recv, cell_sems))
-    sound_copies = start(
-        [
-            remote(sound.at[:, last_rows], sound.at[:, low_pad], sound_sems, 0, {"axial": up_axial}),
-            remote(sound.at[:, first_rows], sound.at[:, high_pad], sound_sems, 1, {"axial": down_axial}),
-        ]
-        + side_halo(sound_send, sound_side, sound_sems)
-    )
-    cell_recv[0] = cell_send[0]
-    sems = halo_sems.at[0]
-    halo_copies = start(
-        side_halo(side_send.at[0], side_recv.at[0], sems)
-        + [
-            remote(field_a.at[:, :, last_rows], field_a.at[:, :, low_pad], sems, 0, {"axial": up_axial}),
-            remote(field_a.at[:, :, first_rows], field_a.at[:, :, high_pad], sems, 1, {"axial": down_axial}),
-        ]
-    )
 
     cell = source[...]
     row_of = jnp.broadcast_to(cell // radial_cells, (rows, flames))
@@ -324,6 +308,28 @@
         jnp.sin(angle), bin_hot, precision=exact, preferred_element_type=F32
     )
 
+    loaded(*[("sound", i) for i in range(tiles)])
+    for side in range(2):
+        for i in range(tiles):
+            sound_send[side, i] = sound[i, padded_side_rows[side], :]
+
+    pl.semaphore_wait(barrier, n_sector + 4)
+
+    start_blocks(cell_send, cell_recv, cell_sems)
+    start_ends(sound.at[:, first_rows], sound.at[:, last_rows], sound_end, sound_sems)
+    start_sides(sound_send, sound_side, sound_sems)
+    cell_recv[0] = cell_send[0]
+
+    loaded(*[("start", i) for i in range(tiles)])
+    loads["rhs"].start()
+    sems = halo_sems.at[0]
+    start_ends(field_a.at[:, :, first_rows], field_a.at[:, :, last_rows], end_recv.at[0], sems)
+    for side in range(2):
+        for c in range(channels):
+            for i in range(tiles):
+                side_send[0, side, c, i] = field_a[c, i, padded_side_rows[side], :]
+    start_sides(side_send.at[0], side_recv.at[0], sems)
+
     def pick(planes):
         high, low = halves(jnp.concatenate(planes, axis=0))
         columns = jnp.dot(
@@ -348,12 +354,11 @@
         )
         high = amounts.astype(BF16).astype(F32)
         flame_send[step] = pack([high, amounts - high])
-        copies = start(blocks(flame_send.at[step], flame_recv.at[step], flame_sems.at[step]))
+        start_blocks(flame_send.at[step], flame_recv.at[step], flame_sems.at[step])
         flame_recv[step, 0] = flame_send[step, 0]
-        return copies[half_blocks:], copies[:half_blocks]
 
     picked_start[...] = pick_field(field_a, inner)
-    near_copies, far_copies = send_flames(picked_start[...], 0)
+    send_flames(picked_start[...], 0)
 
     tile = (azimuth_cells, radial_cells)
     azimuth = lax.broadcasted_iota(I32, tile, 0)
@@ -379,8 +384,8 @@
         k_axial[own_rows(a), :] = 0.5 * (read(sound, own_rows(a)) + read(sound, own_rows(a + 1)))
         return 0
 
-    lax.fori_loop(0, axial_cells, couplings, 0)
-    lax.fori_loop(1, axial_cells, axial_coupling, 0)
+    lax.fori_loop(0, axial_cells, couplings, 0, unroll=True)
+    lax.fori_loop(1, axial_cells, axial_coupling, 0, unroll=True)
 
     loaded("omega", "rhs")
     loads["direct"].start()
@@ -409,34 +414,56 @@
                 total = total + k_rhi * pltpu.roll(x, radial_cells - 1, 1)
                 write(base, c, at, total)
 
-    def make_base(field):
-        lax.fori_loop(
-            1, axial_cells - 1, lambda a, _: (base_rows(field, a, True, True), 0)[1], 0
-        )
-        base_rows(field, 0, False, True)
-        base_rows(field, axial_cells - 1, True, False)
+    def make_base(field, low, high):
+        for a in range(low, high):
+            base_rows(field, a, a > 0, a < axial_cells - 1)
 
     first_axial = axial == 0
     last_axial = axial == n_axial - 1
     first, last = pl.ds(0, azimuth_cells), pl.ds(rows - azimuth_cells, azimuth_cells)
-
-    def add_halo(field, step):
+    whole = pl.ds(0, azimuth_cells)
+
+    edge_rows = 2 * axial_cells + 2 * azimuth_cells
+
+    def signed_sum(terms):
+        return sum(terms[1:modes], terms[0]) - sum(terms[modes + 1 :], terms[modes])
+
+    def add_halo(step):
+        wait_bytes(end_recv.at[step], halo_sems.at[step, 1, 1])
         k_low = k_axial[pl.ds(0, azimuth_cells), :]
         k_high = k_axial[pl.ds(rows, azimuth_cells), :]
+        low_terms, high_terms = [], []
         for c in range(channels):
-            below = jnp.where(first_axial, 0.0, read(field, c, low_pad))
-            write(base, c, first, read(base, c, first) + k_low * below)
-            above = jnp.where(last_axial, 0.0, read(field, c, high_pad))
-            write(base, c, last, read(base, c, last) + k_high * above)
+            below = k_low * jnp.where(first_axial, 0.0, read(end_recv, step, 0, c, whole))
+            above = k_high * jnp.where(last_axial, 0.0, read(end_recv, step, 1, c, whole))
+            write(base, c, first, read(base, c, first) + below)
+            write(base, c, last, read(base, c, last) + above)
+            if step == ITERS - 1:
+                low_terms.append(below * read(direct_tiles, c, first))
+                high_terms.append(above * read(direct_tiles, c, last))
+        wait_bytes(side_recv.at[step], halo_sems.at[step, 1, 0])
         for side in range(2):
             at = side_rows[side]
-            for c in range(channels):
-                for i in range(tiles):
-                    base[c, i, at, :] = (
-                        base[c, i, at, :] + edge[side, i] * side_recv[step, side, c, i]
-                    )
-
-    make_base(field_a)
+            for i in range(tiles):
+                terms = []
+                for c in range(channels):
+                    added = edge[side, i] * side_recv[step, side, c, i]
+                    base[c, i, at, :] = base[c, i, at, :] + added
+                    if step == ITERS - 1:
+                        terms.append(added * direct_tiles[c, i, at, :])
+                if step == ITERS - 1:
+                    edge_own[i, pl.ds(side * axial_cells, axial_cells), :] = scale[
+                        i, at, :
+                    ] * signed_sum(terms)
+        if step == ITERS - 1:
+            for end, at, terms in ((0, first, low_terms), (1, last, high_terms)):
+                write(
+                    edge_own,
+                    pl.ds(2 * axial_cells + end * azimuth_cells, azimuth_cells),
+                    read(scale, at) * signed_sum(terms),
+                )
+
+    make_base(field_a, 0, axial_cells)
 
     def squeeze(recv, group):
         lanes = lax.broadcasted_iota(I32, (8, LANES), 1)
@@ -480,17 +507,18 @@
             for c in range(channels):
                 write(base, c, at, read(base, c, at) - totals[c * chunk : (c + 1) * chunk])
 
-    received(cell_copies[half_blocks:])
+    wait_blocks(cell_recv, cell_sems, near)
     put_hots(near)
-    received(near_copies)
+    wait_blocks(flame_recv.at[0], flame_sems.at[0], near)
     subtract_near(0)
 
-    received(sound_copies)
+    wait_bytes(sound_end, sound_sems.at[1, 1])
+    wait_bytes(sound_side, sound_sems.at[1, 0])
     k_axial[first, :] = 0.5 * (
-        read(sound, first_rows) + jnp.where(first_axial, 0.0, read(sound, low_pad))
+        read(sound, first_rows) + jnp.where(first_axial, 0.0, read(sound_end, 0, whole))
     )
     k_axial[pl.ds(rows, azimuth_cells), :] = 0.5 * (
-        read(sound, last_rows) + jnp.where(last_axial, 0.0, read(sound, high_pad))
+        read(sound, last_rows) + jnp.where(last_axial, 0.0, read(sound_end, 1, whole))
     )
     for side in range(2):
         for i in range(tiles):
@@ -506,13 +534,12 @@
         write(scale, at, RELAX / weights)
         return 0
 
-    lax.fori_loop(0, axial_cells, scales, 0)
+    lax.fori_loop(0, axial_cells, scales, 0, unroll=True)
     all_rows = pl.ds(0, rows)
     picked_scale = pick([read(scale, all_rows)])
 
-    received(cell_copies[:half_blocks])
+    wait_blocks(cell_recv, cell_sems, far)
     row, column = put_hots(far)
-    edge_rows = 2 * axial_cells + 2 * azimuth_cells
     i = lax.broadcasted_iota(I32, (edge_rows, half), 0)
     edge_row = jnp.where(
         i < axial_cells,
@@ -534,16 +561,15 @@
         == jnp.broadcast_to(cell.astype(F32), (half, flames))
     )
 
-    received(halo_copies)
-    add_halo(field_a, 0)
+    add_halo(0)
     picked_base = pick_field(base, all_rows)
 
-    received(far_copies)
+    wait_blocks(flame_recv.at[0], flame_sems.at[0], far)
     parts = halves(squeeze(flame_recv.at[0], far))
     found = jnp.dot(jnp.concatenate(parts, axis=0), match[...], preferred_element_type=F32)
     found = found[:channels] + found[channels:]
     picked = (1.0 - RELAX) * picked_start[...] + picked_scale * (picked_base - found)
-    near_copies, far_copies = send_flames(picked, 1)
+    send_flames(picked, 1)
 
     totals = add_flames(parts, put_edge[...], far)
     for c in range(channels):
@@ -569,14 +595,27 @@
                 + read(scale, at) * (read(base, c, at) - added),
             )
     sems = halo_sems.at[1]
-    halo_copies = start(
-        side_halo(side_send.at[1], side_recv.at[1], sems)
-        + [
-            remote(end_send.at[1], field_b.at[:, :, low_pad], sems, 0, {"axial": up_axial}),
-            remote(end_send.at[0], field_b.at[:, :, high_pad], sems, 1, {"axial": down_axial}),
-        ]
-    )
-
+    start_ends(end_send.at[0], end_send.at[1], end_recv.at[1], sems)
+    start_sides(side_send.at[1], side_recv.at[1], sems)
+
+    loaded("direct")
+    chunk_cells = chunk // azimuth_cells
+
+    def send_sensitivity(top):
+        at = pl.ds(top, chunk)
+        padded_at = pl.ds(top + azimuth_cells, chunk)
+        terms = []
+        for c in range(channels):
+            weight = direct[c, at, :].astype(F32)
+            write(direct_tiles, c, at, weight)
+            terms.append(
+                weight
+                * ((1.0 - RELAX) * read(field_b, c, padded_at) + read(scale, at) * read(base, c, at))
+            )
+        write(sens_own, at, signed_sum(terms))
+        start_partner(sens_own.at[:, at], sens_other.at[:, at], 0)
+
+    done = 0
     for top in range(0, rows, chunk):
         totals = add_flames(parts, put_row[far, top : top + chunk, :], far)
         at = pl.ds(top, chunk)
@@ -589,38 +628,80 @@
                 (1.0 - RELAX) * read(field_a, c, padded_at)
                 + read(scale, at) * (read(base, c, at) - totals[c * chunk : (c + 1) * chunk]),
             )
-
-    make_base(field_b)
-    received(near_copies)
+        ready = (top + chunk) // azimuth_cells
+        ready = axial_cells if ready == axial_cells else ready - 1
+        make_base(field_b, done, ready)
+        done = ready
+        if top:
+            send_sensitivity(top - chunk)
+    send_sensitivity(rows - chunk)
+
+    def direct_at_slots(group):
+        hot = put_row[group].astype(F32)
+        for g in range(2):
+            columns = dot_nt(
+                direct[g * modes : (g + 1) * modes].reshape(modes * rows, radial_cells),
+                put_radial[group],
+            ).reshape(modes, rows, half)
+            slot_direct[group, g * modes : (g + 1) * modes] = jnp.sum(columns * hot[None], axis=1)
+
+    def start_slots(group):
+        products = squeeze(flame_recv.at[1], group) * slot_direct[group]
+        slot_own[group] = jnp.sum(products[:modes], axis=0, keepdims=True) - jnp.sum(
+            products[modes:], axis=0, keepdims=True
+        )
+        start_partner(slot_own.at[group], slot_other.at[group], 1 + group)
+
+    direct_at_slots(near)
+    direct_at_slots(far)
+    wait_blocks(flame_recv.at[1], flame_sems.at[1], near)
+    start_slots(near)
     subtract_near(1)
-    received(halo_copies)
-    add_halo(field_b, 1)
-    loaded("direct")
-    received(far_copies)
+    add_halo(1)
+    start_partner(edge_own, edge_other, 3)
+
+    wait_blocks(flame_recv.at[1], flame_sems.at[1], far)
+    start_slots(far)
     parts = halves(squeeze(flame_recv.at[1], far))
-    sens_copies = []
-    for number, top in enumerate(range(0, rows, chunk)):
+    for top in range(0, rows, chunk):
         totals = add_flames(parts, put_row[far, top : top + chunk, :], far)
         at = pl.ds(top, chunk)
         padded_at = pl.ds(top + azimuth_cells, chunk)
-        sens = jnp.zeros((chunk, radial_cells), F32)
         for c in range(channels):
-            x = (1.0 - RELAX) * read(field_b, c, padded_at) + read(scale, at) * (
+            adjoint[c, at, :] = (1.0 - RELAX) * read(field_b, c, padded_at) + read(scale, at) * (
                 read(base, c, at) - totals[c * chunk : (c + 1) * chunk]
             )
-            adjoint[c, at, :] = x
-            term = x * direct[c, at, :].astype(F32)
-            sens = sens + term if c < modes else sens - term
-        sens_own[at, :] = sens
-        sens_copies += start(
-            [remote(sens_own.at[at], sens_other.at[at], sens_sems, number, {"modes": 1 - my_modes})]
-        )
-    for number, top in enumerate(range(0, rows, chunk)):
-        at = pl.ds(top, chunk)
-        received([sens_copies[number]])
-        sensitivity[at, :] = sens_own[at, :] + sens_other[at, :]
-    for copy in sends:
-        copy.wait_send()
+
+    def slot_sums(group):
+        wait_bytes(slot_other.at[group], sens_sems.at[1, 1 + group])
+        parts = halves(slot_own[group] + slot_other[group])
+        hot = put_row[group]
+        left = jnp.concatenate([hot * part for part in parts], axis=0)
+        totals = jnp.dot(left, put_radial[group], preferred_element_type=F32)
+        return totals[:rows] + totals[rows:]
+
+    wait_bytes(sens_other, sens_sems.at[1, 0])
+    write(
+        sens_sum,
+        all_rows,
+        read(sens_own, all_rows)
+        + read(sens_other, all_rows)
+        - read(scale, all_rows) * slot_sums(near),
+    )
+    wait_bytes(edge_other, sens_sems.at[1, 3])
+    edges = [edge_own[i] + edge_other[i] for i in range(tiles)]
+    for i in range(tiles):
+        for end, at in ((0, first), (1, last)):
+            low = 2 * axial_cells + end * azimuth_cells
+            sens_sum[i, at, :] = sens_sum[i, at, :] + edges[i][low : low + azimuth_cells]
+        for side in range(2):
+            at = side_rows[side]
+            sens_sum[i, at, :] = (
+                sens_sum[i, at, :] + edges[i][side * axial_cells : (side + 1) * axial_cells]
+            )
+    sensitivity[...] = read(sens_sum, all_rows) - read(scale, all_rows) * slot_sums(far)
+    for ref, sem in sent:
+        wait_bytes(ref, sem)
 
 
 def local(
@@ -684,17 +765,26 @@
         vmem((ITERS, 2, channels) + side, F32),
         vmem((ITERS, 2, channels) + side, F32),
         vmem((2, channels, tiles, azimuth_cells, LANES), F32),
+        vmem((ITERS, 2, channels, tiles, azimuth_cells, LANES), F32),
+        vmem((2, tiles, azimuth_cells, LANES), F32),
         vmem((n_sector, 8, LANES), F32),
         vmem((n_sector, 8, LANES), F32),
         vmem((ITERS, n_sector, 8, LANES), F32),
         vmem((ITERS, n_sector, 8, LANES), F32),
-        vmem(plane, F32),
-        vmem(plane, F32),
+        vmem((channels, tiles, rows, LANES), F32),
+        vmem((2, channels, half), F32),
+        vmem((tiles, rows, LANES), F32),
+        vmem((tiles, rows, LANES), F32),
+        vmem((tiles, rows, LANES), F32),
+        vmem((tiles, 2 * (axial_cells + azimuth_cells), LANES), F32),
+        vmem((tiles, 2 * (axial_cells + azimuth_cells), LANES), F32),
+        vmem((2, 1, half), F32),
+        vmem((2, 1, half), F32),
         dma((9 + 2 * tiles,)),
-        dma((2, 4)),
-        dma((ITERS, 2, 4)),
-        dma((2, n_sector)),
-        dma((ITERS, 2, n_sector)),
+        dma((2, 2)),
+        dma((ITERS, 2, 2)),
+        dma((3,)),
+        dma((ITERS, 3)),
         dma((2, 4)),
     ]
     in_hbm = pl.BlockSpec(memory_space=pltpu.HBM)

time: 31.1 us -> 27.5 us (0.88)
  Pallas kernels: 28.7 us -> 25.1 us
    pallas_call x1, Pallas kernels: 28.7 us -> 25.1 us  [local(): pl.pallas_call(functools.partial(kernel, n_sector, n_axial, (modes, axial...]
where the time goes in v3:
time: 27.5 us; the launch traced here: 27.4 us
  Pallas kernels  25.1 us (91%)
  local copies, waits for them, and re-layouts  1.63 us (6%)
  between operations  0.64 us (2%)
    pallas_call x1, Pallas kernels, local(): pl.pallas_call(functools.partial(kernel, n_sector, n_axial, (modes, axial...  25.1 us
    unnamed x2, local copies, waits for them, and re-layouts  1.63 us

profile of v3, /device:TPU:1, one launch (start us, length us, event | category | flops | bytes accessed | tf_op | source)
XLA Modules:
  0.0 27.4 jit_solution(6366490975050122362)
XLA Ops:
  0.6 25.1 %helmholtz_steps.1 = (f32[8,128,256]{2,1,0:T(8,128)S(1)}, f32[128,256]{1,0:T(8,128)S(1)}) custom-call(f32[8,128,256]{2,1,0:T(8,128)} %bitcast.9, f32[8,128,256]{2,1,0:T(8,128)} %bitcast.10, f32[128,256]{1,0:T(8,128)} %bitcast.12, bf16[8,128,256]{2,1,0:T(8,128)(2,1)} %bitcast.11, f32[2,4]{1,0:T(2,128)} %omega_hbm.1, f32[1,512]{1,0:T(1,128)} %gain_hbm.1, ...), custom_call_target="tpu_custom_call" | custom-call | tf_op jit(solution)/shard_map/helmholtz_steps/pallas_call | solution.py:796
  25.8 1.0 %copy.15 = f32[2,4,16,8,256]{4,3,2,1,0:T(8,128)} copy(f32[2,4,16,8,256]{4,3,2,1,0:T(8,128)S(1)} %bitcast.7) | data formatting | bytes 2097152
  26.8 0.7 %copy.16 = f32[16,8,256]{2,1,0:T(8,128)} copy(f32[16,8,256]{2,1,0:T(8,128)S(1)} %bitcast.8) | data formatting | bytes 262144

commit v4 on v3

--- a/solution.py
+++ b/solution.py
@@ -96,6 +96,8 @@
     pick_radial,
     pick_row,
     picked_start,
+    picked_base,
+    edge_pick,
     lane_hot,
     block_hot,
     gain_cos,
@@ -330,12 +332,12 @@
                 side_send[0, side, c, i] = field_a[c, i, padded_side_rows[side], :]
     start_sides(side_send.at[0], side_recv.at[0], sems)
 
-    def pick(planes):
+    def pick(planes, hot=pick_row):
         high, low = halves(jnp.concatenate(planes, axis=0))
         columns = jnp.dot(
             jnp.concatenate([high, low], axis=1), pick_radial[...], preferred_element_type=F32
-        ).reshape(len(planes), rows, flames)
-        return jnp.sum(columns * pick_row[...][None], axis=1)
+        ).reshape(len(planes), hot.shape[0], flames)
+        return jnp.sum(columns * hot[...][None], axis=1)
 
     def pick_field(ref, at):
         return jnp.concatenate(
@@ -365,6 +367,8 @@
     radial = lax.broadcasted_iota(I32, tile, 1)
 
     def own_rows(a):
+        if isinstance(a, int):
+            return pl.ds(a * azimuth_cells, azimuth_cells)
         return pl.ds(pl.multiple_of(a * azimuth_cells, azimuth_cells), azimuth_cells)
 
     def couplings(a, _):
@@ -392,12 +396,13 @@
     omega_real = [omega[0, m] for m in range(modes)]
     omega_imag = [omega[1, m] for m in range(modes)]
 
-    def base_rows(field, a, low, high):
+    def base_rows(field, a, modes_here):
+        low, high = a > 0, a < axial_cells - 1
         at, mid, top = own_rows(a), own_rows(a + 1), own_rows(a + 2)
         k_slo, k_shi, k_rlo, k_rhi = (k_rest[i, at, :] for i in range(4))
         k_alo = k_axial[at, :] if low else None
         k_ahi = k_axial[mid, :] if high else None
-        for m in range(modes):
+        for m in modes_here:
             real, imag = read(field, m, mid), read(field, modes + m, mid)
             for c, x, mass in (
                 (m, real, omega_real[m] * real - omega_imag[m] * imag),
@@ -416,7 +421,7 @@
 
     def make_base(field, low, high):
         for a in range(low, high):
-            base_rows(field, a, a > 0, a < axial_cells - 1)
+            base_rows(field, a, range(modes))
 
     first_axial = axial == 0
     last_axial = axial == n_axial - 1
@@ -432,22 +437,25 @@
         wait_bytes(end_recv.at[step], halo_sems.at[step, 1, 1])
         k_low = k_axial[pl.ds(0, azimuth_cells), :]
         k_high = k_axial[pl.ds(rows, azimuth_cells), :]
-        low_terms, high_terms = [], []
+        low_terms, high_terms, planes = [], [], [[] for _ in range(channels)]
         for c in range(channels):
             below = k_low * jnp.where(first_axial, 0.0, read(end_recv, step, 0, c, whole))
             above = k_high * jnp.where(last_axial, 0.0, read(end_recv, step, 1, c, whole))
             write(base, c, first, read(base, c, first) + below)
             write(base, c, last, read(base, c, last) + above)
+            planes[c] += [below, above]
             if step == ITERS - 1:
                 low_terms.append(below * read(direct_tiles, c, first))
                 high_terms.append(above * read(direct_tiles, c, last))
         wait_bytes(side_recv.at[step], halo_sems.at[step, 1, 0])
         for side in range(2):
             at = side_rows[side]
+            sides = [[] for _ in range(channels)]
             for i in range(tiles):
                 terms = []
                 for c in range(channels):
                     added = edge[side, i] * side_recv[step, side, c, i]
+                    sides[c].append(added)
                     base[c, i, at, :] = base[c, i, at, :] + added
                     if step == ITERS - 1:
                         terms.append(added * direct_tiles[c, i, at, :])
@@ -455,6 +463,10 @@
                     edge_own[i, pl.ds(side * axial_cells, axial_cells), :] = scale[
                         i, at, :
                     ] * signed_sum(terms)
+            for c in range(channels):
+                planes[c].insert(side, jnp.concatenate(sides[c], axis=1))
+        if step < ITERS - 1:
+            return [jnp.concatenate(parts, axis=0) for parts in planes]
         if step == ITERS - 1:
             for end, at, terms in ((0, first, low_terms), (1, last, high_terms)):
                 write(
@@ -463,7 +475,15 @@
                     read(scale, at) * signed_sum(terms),
                 )
 
-    make_base(field_a, 0, axial_cells)
+    all_rows = pl.ds(0, rows)
+    real_base, imag_base = [], []
+    for m in range(modes):
+        for a in range(axial_cells):
+            base_rows(field_a, a, [m])
+        pair = pick([read(base, m, all_rows), read(base, modes + m, all_rows)])
+        real_base.append(pair[0:1])
+        imag_base.append(pair[1:2])
+    picked_base[...] = jnp.concatenate(real_base + imag_base, axis=0)
 
     def squeeze(recv, group):
         lanes = lax.broadcasted_iota(I32, (8, LANES), 1)
@@ -499,48 +519,7 @@
 
     chunk = rows // 4
 
-    def subtract_near(step):
-        parts = halves(squeeze(flame_recv.at[step], near))
-        for top in range(0, rows, chunk):
-            at = pl.ds(top, chunk)
-            totals = add_flames(parts, put_row[near, top : top + chunk, :], near)
-            for c in range(channels):
-                write(base, c, at, read(base, c, at) - totals[c * chunk : (c + 1) * chunk])
-
-    wait_blocks(cell_recv, cell_sems, near)
-    put_hots(near)
-    wait_blocks(flame_recv.at[0], flame_sems.at[0], near)
-    subtract_near(0)
-
-    wait_bytes(sound_end, sound_sems.at[1, 1])
-    wait_bytes(sound_side, sound_sems.at[1, 0])
-    k_axial[first, :] = 0.5 * (
-        read(sound, first_rows) + jnp.where(first_axial, 0.0, read(sound_end, 0, whole))
-    )
-    k_axial[pl.ds(rows, azimuth_cells), :] = 0.5 * (
-        read(sound, last_rows) + jnp.where(last_axial, 0.0, read(sound_end, 1, whole))
-    )
-    for side in range(2):
-        for i in range(tiles):
-            edge[side, i] = 0.5 * (sound[i, padded_side_rows[side], :] + sound_side[side, i])
-
-    def scales(a, _):
-        at = own_rows(a)
-        low = jnp.broadcast_to(read(edge, 0, pl.ds(a, 1)), tile)
-        high = jnp.broadcast_to(read(edge, 1, pl.ds(a, 1)), tile)
-        weights = k_axial[at, :] + k_axial[own_rows(a + 1), :] + k_rest[2, at, :] + k_rest[3, at, :]
-        weights = weights + jnp.where(azimuth == 0, low, k_rest[0, at, :])
-        weights = weights + jnp.where(azimuth == azimuth_cells - 1, high, k_rest[1, at, :])
-        write(scale, at, RELAX / weights)
-        return 0
-
-    lax.fori_loop(0, axial_cells, scales, 0, unroll=True)
-    all_rows = pl.ds(0, rows)
-    picked_scale = pick([read(scale, all_rows)])
-
-    wait_blocks(cell_recv, cell_sems, far)
-    row, column = put_hots(far)
-    i = lax.broadcasted_iota(I32, (edge_rows, half), 0)
+    i = lax.broadcasted_iota(I32, (edge_rows, LANES), 0)
     edge_row = jnp.where(
         i < axial_cells,
         i * azimuth_cells,
@@ -553,25 +532,77 @@
                 i - 2 * axial_cells - 2 * azimuth_cells + rows,
             ),
         ),
-    )
-    put_edge[...] = one_hot(edge_row.astype(F32) == jnp.broadcast_to(row, (edge_rows, half)))
-    upright = jnp.broadcast_to(row * radial_cells + column, (LANES, half)).T
-    match[...] = one_hot(
-        jnp.concatenate([upright] * (flames // LANES), axis=1)
-        == jnp.broadcast_to(cell.astype(F32), (half, flames))
-    )
-
-    add_halo(0)
-    picked_base = pick_field(base, all_rows)
+    ).astype(F32)
+    flame_row = (cell // radial_cells).astype(F32)
+    edge_pick[...] = jnp.where(
+        jnp.concatenate([edge_row] * (flames // LANES), axis=1)
+        == jnp.broadcast_to(flame_row, (edge_rows, flames)),
+        1.0,
+        0.0,
+    )
+
+    def all_hots(group):
+        row, column = put_hots(group)
+        put_edge[group] = one_hot(
+            jnp.concatenate([edge_row] * (half // LANES), axis=1)
+            == jnp.broadcast_to(row, (edge_rows, half))
+        )
+        upright = jnp.broadcast_to(row * radial_cells + column, (LANES, half)).T
+        match[group] = one_hot(
+            jnp.concatenate([upright] * (flames // LANES), axis=1)
+            == jnp.broadcast_to(cell.astype(F32), (half, flames))
+        )
+
+    def found_at_flames(parts, group):
+        found = jnp.dot(jnp.concatenate(parts, axis=0), match[group], preferred_element_type=F32)
+        return found[:channels] + found[channels:]
+
+    wait_blocks(cell_recv, cell_sems, near)
+    all_hots(near)
+
+    wait_bytes(sound_end, sound_sems.at[1, 1])
+    wait_bytes(sound_side, sound_sems.at[1, 0])
+    k_axial[first, :] = 0.5 * (
+        read(sound, first_rows) + jnp.where(first_axial, 0.0, read(sound_end, 0, whole))
+    )
+    k_axial[pl.ds(rows, azimuth_cells), :] = 0.5 * (
+        read(sound, last_rows) + jnp.where(last_axial, 0.0, read(sound_end, 1, whole))
+    )
+    for side in range(2):
+        for i in range(tiles):
+            edge[side, i] = 0.5 * (sound[i, padded_side_rows[side], :] + sound_side[side, i])
+
+    def scales(a, _):
+        at = own_rows(a)
+        low = jnp.broadcast_to(read(edge, 0, pl.ds(a, 1)), tile)
+        high = jnp.broadcast_to(read(edge, 1, pl.ds(a, 1)), tile)
+        weights = k_axial[at, :] + k_axial[own_rows(a + 1), :] + k_rest[2, at, :] + k_rest[3, at, :]
+        weights = weights + jnp.where(azimuth == 0, low, k_rest[0, at, :])
+        weights = weights + jnp.where(azimuth == azimuth_cells - 1, high, k_rest[1, at, :])
+        write(scale, at, RELAX / weights)
+        return 0
+
+    lax.fori_loop(0, axial_cells, scales, 0, unroll=True)
+    picked_scale = pick([read(scale, all_rows)])
+
+    wait_blocks(cell_recv, cell_sems, far)
+    all_hots(far)
+    wait_blocks(flame_recv.at[0], flame_sems.at[0], near)
+    near_parts = halves(squeeze(flame_recv.at[0], near))
+    found_near = found_at_flames(near_parts, near)
+    planes = add_halo(0)
+    inside = picked_base[...] - found_near + pick(planes, edge_pick)
+
+    edge_totals = add_flames(near_parts, put_edge[near], near)
 
     wait_blocks(flame_recv.at[0], flame_sems.at[0], far)
     parts = halves(squeeze(flame_recv.at[0], far))
-    found = jnp.dot(jnp.concatenate(parts, axis=0), match[...], preferred_element_type=F32)
-    found = found[:channels] + found[channels:]
-    picked = (1.0 - RELAX) * picked_start[...] + picked_scale * (picked_base - found)
+    picked = (1.0 - RELAX) * picked_start[...] + picked_scale * (
+        inside - found_at_flames(parts, far)
+    )
     send_flames(picked, 1)
 
-    totals = add_flames(parts, put_edge[...], far)
+    totals = edge_totals + add_flames(parts, put_edge[far], far)
     for c in range(channels):
         here = c * edge_rows
         for side in range(2):
@@ -617,7 +648,8 @@
 
     done = 0
     for top in range(0, rows, chunk):
-        totals = add_flames(parts, put_row[far, top : top + chunk, :], far)
+        totals = add_flames(near_parts, put_row[near, top : top + chunk, :], near)
+        totals = totals + add_flames(parts, put_row[far, top : top + chunk, :], far)
         at = pl.ds(top, chunk)
         padded_at = pl.ds(top + azimuth_cells, chunk)
         for c in range(channels):
@@ -645,26 +677,23 @@
             ).reshape(modes, rows, half)
             slot_direct[group, g * modes : (g + 1) * modes] = jnp.sum(columns * hot[None], axis=1)
 
-    def start_slots(group):
-        products = squeeze(flame_recv.at[1], group) * slot_direct[group]
+    direct_at_slots(near)
+    direct_at_slots(far)
+    add_halo(1)
+    start_partner(edge_own, edge_other, 2)
+    parts = []
+    for group in (near, far):
+        wait_blocks(flame_recv.at[1], flame_sems.at[1], group)
+        amounts = squeeze(flame_recv.at[1], group)
+        products = amounts * slot_direct[group]
         slot_own[group] = jnp.sum(products[:modes], axis=0, keepdims=True) - jnp.sum(
             products[modes:], axis=0, keepdims=True
         )
-        start_partner(slot_own.at[group], slot_other.at[group], 1 + group)
-
-    direct_at_slots(near)
-    direct_at_slots(far)
-    wait_blocks(flame_recv.at[1], flame_sems.at[1], near)
-    start_slots(near)
-    subtract_near(1)
-    add_halo(1)
-    start_partner(edge_own, edge_other, 3)
-
-    wait_blocks(flame_recv.at[1], flame_sems.at[1], far)
-    start_slots(far)
-    parts = halves(squeeze(flame_recv.at[1], far))
+        parts.append(halves(amounts))
+    start_partner(slot_own, slot_other, 1)
     for top in range(0, rows, chunk):
-        totals = add_flames(parts, put_row[far, top : top + chunk, :], far)
+        totals = add_flames(parts[near], put_row[near, top : top + chunk, :], near)
+        totals = totals + add_flames(parts[far], put_row[far, top : top + chunk, :], far)
         at = pl.ds(top, chunk)
         padded_at = pl.ds(top + azimuth_cells, chunk)
         for c in range(channels):
@@ -672,23 +701,9 @@
                 read(base, c, at) - totals[c * chunk : (c + 1) * chunk]
             )
 
-    def slot_sums(group):
-        wait_bytes(slot_other.at[group], sens_sems.at[1, 1 + group])
-        parts = halves(slot_own[group] + slot_other[group])
-        hot = put_row[group]
-        left = jnp.concatenate([hot * part for part in parts], axis=0)
-        totals = jnp.dot(left, put_radial[group], preferred_element_type=F32)
-        return totals[:rows] + totals[rows:]
-
     wait_bytes(sens_other, sens_sems.at[1, 0])
-    write(
-        sens_sum,
-        all_rows,
-        read(sens_own, all_rows)
-        + read(sens_other, all_rows)
-        - read(scale, all_rows) * slot_sums(near),
-    )
-    wait_bytes(edge_other, sens_sems.at[1, 3])
+    write(sens_sum, all_rows, read(sens_own, all_rows) + read(sens_other, all_rows))
+    wait_bytes(edge_other, sens_sems.at[1, 2])
     edges = [edge_own[i] + edge_other[i] for i in range(tiles)]
     for i in range(tiles):
         for end, at in ((0, first), (1, last)):
@@ -699,9 +714,28 @@
             sens_sum[i, at, :] = (
                 sens_sum[i, at, :] + edges[i][side * axial_cells : (side + 1) * axial_cells]
             )
-    sensitivity[...] = read(sens_sum, all_rows) - read(scale, all_rows) * slot_sums(far)
+    wait_bytes(slot_other, sens_sems.at[1, 1])
+    slot_totals = 0.0
+    for group in (near, far):
+        left = jnp.concatenate(
+            [put_row[group] * part for part in halves(slot_own[group] + slot_other[group])], axis=0
+        )
+        totals = jnp.dot(left, put_radial[group], preferred_element_type=F32)
+        slot_totals = slot_totals + totals[:rows] + totals[rows:]
+    sensitivity[...] = read(sens_sum, all_rows) - read(scale, all_rows) * slot_totals
     for ref, sem in sent:
         wait_bytes(ref, sem)
+
+
+def hand_over(adjoint_in, sensitivity_in, adjoint_out, sensitivity_out, sems):
+    copies = [
+        pltpu.make_async_copy(sensitivity_in, sensitivity_out, sems.at[0]),
+        pltpu.make_async_copy(adjoint_in, adjoint_out, sems.at[1]),
+    ]
+    for copy in copies:
+        copy.start()
+    for copy in copies:
+        copy.wait()
 
 
 def local(
@@ -752,14 +786,16 @@
         vmem((2 * radial_cells, flames), BF16),
         vmem((rows, flames), F32),
         vmem((channels, flames), F32),
+        vmem((channels, flames), F32),
+        vmem((2 * (axial_cells + azimuth_cells), flames), F32),
         vmem((LANES, flames), BF16),
         vmem((n_sector, flames), F32),
         vmem((modes, flames), F32),
         vmem((modes, flames), F32),
         vmem((2, rows, half), BF16),
-        vmem((2 * (axial_cells + azimuth_cells), half), BF16),
+        vmem((2, 2 * (axial_cells + azimuth_cells), half), BF16),
         vmem((2, half, radial_cells), BF16),
-        vmem((half, flames), BF16),
+        vmem((2, half, flames), BF16),
         vmem((2,) + side, F32),
         vmem((2,) + side, F32),
         vmem((ITERS, 2, channels) + side, F32),
@@ -785,7 +821,7 @@
         dma((ITERS, 2, 2)),
         dma((3,)),
         dma((ITERS, 3)),
-        dma((2, 4)),
+        dma((2, 3)),
     ]
     in_hbm = pl.BlockSpec(memory_space=pltpu.HBM)
 
@@ -818,6 +854,17 @@
         stay(injector_sector.reshape(1, flames)),
         stay(injector_cell),
     )
+    adjoint, sensitivity = pl.pallas_call(
+        hand_over,
+        out_shape=(jax.ShapeDtypeStruct(block, F32), jax.ShapeDtypeStruct(plane, F32)),
+        in_specs=[in_vmem] * 2,
+        out_specs=(in_hbm, in_hbm),
+        scratch_shapes=[dma((2,))],
+        name="hand_over",
+    )(
+        pltpu.with_memory_space_constraint(adjoint, pltpu.VMEM),
+        pltpu.with_memory_space_constraint(sensitivity, pltpu.VMEM),
+    )
     return adjoint.reshape(rhs.shape), sensitivity.reshape(sound_sq.shape)
 
 

time: 27.5 us -> 26.6 us (0.967)
  local copies, waits for them, and re-layouts: 1.63 us -> 0 us
  Pallas kernels: 25.1 us -> 25.8 us
    unnamed x2 -> x0, local copies, waits for them, and re-layouts: 1.63 us -> none
    pallas_call x0 -> x1, Pallas kernels: none -> 1.03 us  [local(): pl.pallas_call(hand_over, out_shape=(jax.ShapeDtypeStruct(block, F32), ja...]
    pallas_call x1, Pallas kernels: 25.1 us -> 24.8 us  [local(): pl.pallas_call(functools.partial(kernel, n_sector, n_axial, (modes, axial...]
where the time goes in v4:
time: 26.6 us; the launch traced here: 26.5 us
  Pallas kernels  25.8 us (97%)
  between operations  0.64 us (2%)
    pallas_call x1, Pallas kernels, local(): pl.pallas_call(functools.partial(kernel, n_sector, n_axial, (modes, axial...  24.8 us
    pallas_call x1, Pallas kernels, local(): pl.pallas_call(hand_over, out_shape=(jax.ShapeDtypeStruct(block, F32), ja...  1.03 us

profile of v4, /device:TPU:1, one launch (start us, length us, event | category | flops | bytes accessed | tf_op | source)
XLA Modules:
  0.0 26.5 jit_solution(11964638075679973082)
XLA Ops:
  0.6 24.8 %helmholtz_steps.1 = (f32[8,128,256]{2,1,0:T(8,128)S(1)}, f32[128,256]{1,0:T(8,128)S(1)}) custom-call(f32[8,128,256]{2,1,0:T(8,128)} %bitcast.7, f32[8,128,256]{2,1,0:T(8,128)} %bitcast.8, f32[128,256]{1,0:T(8,128)} %bitcast.10, bf16[8,128,256]{2,1,0:T(8,128)(2,1)} %bitcast.9, f32[2,4]{1,0:T(2,128)} %omega_hbm.1, f32[1,512]{1,0:T(1,128)} %gain_hbm.1, ...), custom_call_target="tpu_custom_call" | custom-call | tf_op jit(solution)/shard_map/helmholtz_steps/pallas_call | solution.py:832
  25.4 1.0 %hand_over.1 = (f32[8,128,256]{2,1,0:T(8,128)}, f32[128,256]{1,0:T(8,128)}) custom-call(f32[8,128,256]{2,1,0:T(8,128)S(1)} %get-tuple-element.6.adjoint_in, f32[128,256]{1,0:T(8,128)S(1)} %get-tuple-element.7.sensitivity_in), custom_call_target="tpu_custom_call" | custom-call | tf_op jit(solution)/shard_map/hand_over/pallas_call | solution.py:857

commit v5 on v4

--- a/solution.py
+++ b/solution.py
@@ -75,7 +75,11 @@
     sector_hbm,
     target_hbm,
     adjoint,
-    sensitivity,
+    sens_sum,
+    scale,
+    slot_sum,
+    put_row,
+    put_radial,
     rhs,
     field_a,
     field_b,
@@ -89,7 +93,6 @@
     sector,
     target,
     base,
-    scale,
     k_axial,
     k_rest,
     edge,
@@ -102,9 +105,7 @@
     block_hot,
     gain_cos,
     gain_sin,
-    put_row,
     put_edge,
-    put_radial,
     match,
     sound_send,
     sound_side,
@@ -121,7 +122,6 @@
     slot_direct,
     sens_own,
     sens_other,
-    sens_sum,
     edge_own,
     edge_other,
     slot_own,
@@ -284,6 +284,28 @@
         pl.ds(azimuth_cells + row, axial_cells, azimuth_cells) for row in (0, azimuth_cells - 1)
     ]
 
+    loaded(*[("sound", i) for i in range(tiles)])
+    for side in range(2):
+        for i in range(tiles):
+            sound_send[side, i] = sound[i, padded_side_rows[side], :]
+
+    pl.semaphore_wait(barrier, n_sector + 4)
+
+    start_blocks(cell_send, cell_recv, cell_sems)
+    start_ends(sound.at[:, first_rows], sound.at[:, last_rows], sound_end, sound_sems)
+    start_sides(sound_send, sound_side, sound_sems)
+    cell_recv[0] = cell_send[0]
+
+    loaded(*[("start", i) for i in range(tiles)])
+    loads["rhs"].start()
+    sems = halo_sems.at[0]
+    for side in range(2):
+        for c in range(channels):
+            for i in range(tiles):
+                side_send[0, side, c, i] = field_a[c, i, padded_side_rows[side], :]
+    start_sides(side_send.at[0], side_recv.at[0], sems)
+    start_ends(field_a.at[:, :, first_rows], field_a.at[:, :, last_rows], end_recv.at[0], sems)
+
     cell = source[...]
     row_of = jnp.broadcast_to(cell // radial_cells, (rows, flames))
     pick_row[...] = jnp.where(lax.broadcasted_iota(I32, (rows, flames), 0) == row_of, 1.0, 0.0)
@@ -309,28 +331,6 @@
     gain_sin[...] = -gains * jnp.dot(
         jnp.sin(angle), bin_hot, precision=exact, preferred_element_type=F32
     )
-
-    loaded(*[("sound", i) for i in range(tiles)])
-    for side in range(2):
-        for i in range(tiles):
-            sound_send[side, i] = sound[i, padded_side_rows[side], :]
-
-    pl.semaphore_wait(barrier, n_sector + 4)
-
-    start_blocks(cell_send, cell_recv, cell_sems)
-    start_ends(sound.at[:, first_rows], sound.at[:, last_rows], sound_end, sound_sems)
-    start_sides(sound_send, sound_side, sound_sems)
-    cell_recv[0] = cell_send[0]
-
-    loaded(*[("start", i) for i in range(tiles)])
-    loads["rhs"].start()
-    sems = halo_sems.at[0]
-    start_ends(field_a.at[:, :, first_rows], field_a.at[:, :, last_rows], end_recv.at[0], sems)
-    for side in range(2):
-        for c in range(channels):
-            for i in range(tiles):
-                side_send[0, side, c, i] = field_a[c, i, padded_side_rows[side], :]
-    start_sides(side_send.at[0], side_recv.at[0], sems)
 
     def pick(planes, hot=pick_row):
         high, low = halves(jnp.concatenate(planes, axis=0))
@@ -597,12 +597,8 @@
 
     wait_blocks(flame_recv.at[0], flame_sems.at[0], far)
     parts = halves(squeeze(flame_recv.at[0], far))
-    picked = (1.0 - RELAX) * picked_start[...] + picked_scale * (
-        inside - found_at_flames(parts, far)
-    )
-    send_flames(picked, 1)
-
     totals = edge_totals + add_flames(parts, put_edge[far], far)
+    sems = halo_sems.at[1]
     for c in range(channels):
         here = c * edge_rows
         for side in range(2):
@@ -614,7 +610,9 @@
                 side_send[1, side, c, i] = (1.0 - RELAX) * side_send[0, side, c, i] + scale[
                     i, side_rows[side], :
                 ] * (base[c, i, side_rows[side], :] - added)
-        here = here + 2 * axial_cells
+    start_sides(side_send.at[1], side_recv.at[1], sems)
+    for c in range(channels):
+        here = c * edge_rows + 2 * axial_cells
         for end, at, padded_at in ((0, first, first_rows), (1, last, last_rows)):
             added = totals[here + end * azimuth_cells : here + (end + 1) * azimuth_cells]
             write(
@@ -625,9 +623,12 @@
                 (1.0 - RELAX) * read(field_a, c, padded_at)
                 + read(scale, at) * (read(base, c, at) - added),
             )
-    sems = halo_sems.at[1]
     start_ends(end_send.at[0], end_send.at[1], end_recv.at[1], sems)
-    start_sides(side_send.at[1], side_recv.at[1], sems)
+
+    picked = (1.0 - RELAX) * picked_start[...] + picked_scale * (
+        inside - found_at_flames(parts, far)
+    )
+    send_flames(picked, 1)
 
     loaded("direct")
     chunk_cells = chunk // azimuth_cells
@@ -715,27 +716,39 @@
                 sens_sum[i, at, :] + edges[i][side * axial_cells : (side + 1) * axial_cells]
             )
     wait_bytes(slot_other, sens_sems.at[1, 1])
+    slot_sum[...] = slot_own[...] + slot_other[...]
+    for ref, sem in sent:
+        wait_bytes(ref, sem)
+
+
+def hand_over(
+    adjoint,
+    sens_sum,
+    scale,
+    slot_sum,
+    put_row,
+    put_radial,
+    adjoint_out,
+    sensitivity_out,
+    sensitivity,
+    sems,
+):
+    rows = put_row.shape[1]
+    adjoint_copy = pltpu.make_async_copy(adjoint, adjoint_out, sems.at[0])
+    adjoint_copy.start()
     slot_totals = 0.0
-    for group in (near, far):
+    for group in range(2):
         left = jnp.concatenate(
-            [put_row[group] * part for part in halves(slot_own[group] + slot_other[group])], axis=0
+            [put_row[group] * part for part in halves(slot_sum[group])], axis=0
         )
         totals = jnp.dot(left, put_radial[group], preferred_element_type=F32)
         slot_totals = slot_totals + totals[:rows] + totals[rows:]
+    all_rows = pl.ds(0, rows)
     sensitivity[...] = read(sens_sum, all_rows) - read(scale, all_rows) * slot_totals
-    for ref, sem in sent:
-        wait_bytes(ref, sem)
-
-
-def hand_over(adjoint_in, sensitivity_in, adjoint_out, sensitivity_out, sems):
-    copies = [
-        pltpu.make_async_copy(sensitivity_in, sensitivity_out, sems.at[0]),
-        pltpu.make_async_copy(adjoint_in, adjoint_out, sems.at[1]),
-    ]
-    for copy in copies:
-        copy.start()
-    for copy in copies:
-        copy.wait()
+    sensitivity_copy = pltpu.make_async_copy(sensitivity, sensitivity_out, sems.at[1])
+    sensitivity_copy.start()
+    sensitivity_copy.wait()
+    adjoint_copy.wait()
 
 
 def local(
@@ -779,7 +792,6 @@
         vmem((1, flames), I32),
         vmem((1, flames), I32),
         vmem((channels, tiles, rows, LANES), F32),
-        vmem((tiles, rows, LANES), F32),
         vmem((rows + azimuth_cells, radial_cells), F32),
         vmem((4,) + plane, F32),
         vmem((2,) + side, F32),
@@ -792,9 +804,7 @@
         vmem((n_sector, flames), F32),
         vmem((modes, flames), F32),
         vmem((modes, flames), F32),
-        vmem((2, rows, half), BF16),
         vmem((2, 2 * (axial_cells + azimuth_cells), half), BF16),
-        vmem((2, half, radial_cells), BF16),
         vmem((2, half, flames), BF16),
         vmem((2,) + side, F32),
         vmem((2,) + side, F32),
@@ -811,7 +821,6 @@
         vmem((2, channels, half), F32),
         vmem((tiles, rows, LANES), F32),
         vmem((tiles, rows, LANES), F32),
-        vmem((tiles, rows, LANES), F32),
         vmem((tiles, 2 * (axial_cells + azimuth_cells), LANES), F32),
         vmem((tiles, 2 * (axial_cells + azimuth_cells), LANES), F32),
         vmem((2, 1, half), F32),
@@ -829,13 +838,20 @@
         return pltpu.with_memory_space_constraint(array, pltpu.HBM)
 
     in_vmem = pl.BlockSpec(memory_space=pltpu.VMEM)
-    adjoint, sensitivity = pl.pallas_call(
+    results = pl.pallas_call(
         functools.partial(
             kernel, n_sector, n_axial, (modes, axial_cells, azimuth_cells, radial_cells)
         ),
-        out_shape=(jax.ShapeDtypeStruct(block, F32), jax.ShapeDtypeStruct(plane, F32)),
+        out_shape=(
+            jax.ShapeDtypeStruct(block, F32),
+            jax.ShapeDtypeStruct((tiles, rows, LANES), F32),
+            jax.ShapeDtypeStruct((tiles, rows, LANES), F32),
+            jax.ShapeDtypeStruct((2, 1, half), F32),
+            jax.ShapeDtypeStruct((2, rows, half), BF16),
+            jax.ShapeDtypeStruct((2, half, radial_cells), BF16),
+        ),
         in_specs=[in_hbm] * 11,
-        out_specs=(in_vmem, in_vmem),
+        out_specs=(in_vmem,) * 6,
         scratch_shapes=scratch,
         compiler_params=pltpu.CompilerParams(
             collective_id=0, has_side_effects=True, vmem_limit_bytes=40 * 1024 * 1024
@@ -857,14 +873,12 @@
     adjoint, sensitivity = pl.pallas_call(
         hand_over,
         out_shape=(jax.ShapeDtypeStruct(block, F32), jax.ShapeDtypeStruct(plane, F32)),
-        in_specs=[in_vmem] * 2,
+        in_specs=[in_vmem] * 6,
         out_specs=(in_hbm, in_hbm),
-        scratch_shapes=[dma((2,))],
+        scratch_shapes=[vmem(plane, F32), dma((2,))],
+        compiler_params=pltpu.CompilerParams(vmem_limit_bytes=20 * 1024 * 1024),
         name="hand_over",
-    )(
-        pltpu.with_memory_space_constraint(adjoint, pltpu.VMEM),
-        pltpu.with_memory_space_constraint(sensitivity, pltpu.VMEM),
-    )
+    )(*[pltpu.with_memory_space_constraint(result, pltpu.VMEM) for result in results])
     return adjoint.reshape(rhs.shape), sensitivity.reshape(sound_sq.shape)
 
 

time: 26.6 us -> 26.3 us (0.989)
  Pallas kernels: 25.8 us -> 25.5 us
    pallas_call x1, Pallas kernels: 24.8 us -> 24.4 us  [local(): pl.pallas_call(functools.partial(kernel, n_sector, n_axial, (modes, axial...]
where the time goes in v5:
time: 26.3 us; the launch traced here: 26.1 us
  Pallas kernels  25.5 us (97%)
  between operations  0.64 us (2%)
    pallas_call x1, Pallas kernels, local(): pl.pallas_call(functools.partial(kernel, n_sector, n_axial, (modes, axial...  24.4 us
    pallas_call x1, Pallas kernels, local(): pl.pallas_call(hand_over, out_shape=(jax.ShapeDtypeStruct(block, F32), ja...  1.06 us

profile of v5, /device:TPU:1, one launch (start us, length us, event | category | flops | bytes accessed | tf_op | source)
XLA Modules:
  0.0 26.1 jit_solution(11978562715237501557)
XLA Ops:
  0.6 24.4 %helmholtz_steps.1 = (f32[8,128,256]{2,1,0:T(8,128)S(1)}, f32[2,128,128]{2,1,0:T(8,128)S(1)}, f32[2,128,128]{2,1,0:T(8,128)S(1)}, f32[2,1,768]{2,1,0:T(1,128)S(1...) custom-call(f32[8,128,256]{2,1,0:T(8,128)} %bitcast.7, f32[8,128,256]{2,1,0:T(8,128)} %bitcast.8, ...), custom_call_target="tpu_custom_call" | custom-call | tf_op jit(solution)/shard_map/helmholtz_steps/pallas_call | solution.py:841
  25.0 1.1 %hand_over.1 = (f32[8,128,256]{2,1,0:T(8,128)}, f32[128,256]{1,0:T(8,128)}) custom-call(f32[8,128,256]{2,1,0:T(8,128)S(1)} %get-tuple-element.10.adjoint, f32[2,128,128]{2,1,0:T(8,128)S(1)} %get-tuple-element.11.sens_sum, f32[2,128,128]{2,1,0:T(8,128)S(1)} %get-tuple-element.12.scale, f32[2,1,768]{2,1,0:T(1,128)S(1)} %get-tuple-element.13.slot_sum, ...), custom_call_target="tpu_custom_call" | custom-call | tf_op jit(solution)/shard_map/hand_over/pallas_call | solution.py:873
